TPU v7x, 32 devices: a whole 2x2x4 slice. The times are simulated.
32 devices in a mesh: gx: 4 (over y, x), gy: 4 (over z), gz: 2 (over core).
Axes of the slice: x: 2, y: 2, z: 4, core: 2. Of those that a mesh axis runs over, the one named last changes fastest.
Arguments:
- solution_old: float32 [128, 32, 1024], P(('gx', 'gy', 'gz')), may hold values from -6 to 6
- right_side: float32 [128, 32, 1024], P(('gx', 'gy', 'gz')), may hold values from -6 to 6
- acoef: float32 [128, 32, 1024], P(('gx', 'gy', 'gz')), may hold values from 0.05 to 1
- bcoef: float32 [128, 32, 1024], P(('gx', 'gy', 'gz')), may hold values from 0.25 to 4
- corners: int32 [3, 128], replicated, may hold values from 0 to 224, as said below
Outputs:
- solution: float32 [128, 128, 256], P('gx', 'gy', 'gz')
- residual: float32 [128, 128, 256], P('gx', 'gy', 'gz')
Inputs may be any that keep to these rules, and one draw needn't show every extreme that they name: `corners`: each corner is a multiple of 32 in every dimension and the boxes tile the level one to one. The new owner of a box, the device whose block of 32 x 32 x 128 cells holds its corner, has the same gx and gz indices as the device that holds its row. At most one box moves from one device to any other device, and at most min(3, 3) boxes leave or reach one device; in each group of devices with one gx and one gz index, one device swaps a box with each of that many others, and every other device of the group passes one box on along a cycle through them.
All inputs are finite; a program needn't handle non-finite values.
Results may differ from a plain program's by a relative error of at most 0.00002.
Values sent between devices are 32-bit elements; how exact they have to be, the bound alone decides.
A program may use at most 64 MiB of HBM per device.

v0:
```python
import jax
import jax.numpy as jnp
from jax import lax
from jax.sharding import PartitionSpec as P

BXB = 1
BYB = 1
BZB = 4
SWEEPS = 2


def extended(block, sides, width):
    for axis, dim in sides:
        count = lax.axis_size(axis)
        forward = [(i, i + 1) for i in range(count - 1)]
        backward = [(target, source) for source, target in forward]
        low = lax.ppermute(
            lax.slice_in_dim(block, block.shape[dim] - width, None, axis=dim), axis, forward
        )
        high = lax.ppermute(lax.slice_in_dim(block, 0, width, axis=dim), axis, backward)
        block = jnp.concatenate([low, block, high], axis=dim)
    return block


def face_coefs(padded):
    face_x = 0.5 * (padded[1:, 1:-1, 1:-1] + padded[:-1, 1:-1, 1:-1])
    face_y = 0.5 * (padded[1:-1, 1:, 1:-1] + padded[1:-1, :-1, 1:-1])
    face_z = 0.5 * (padded[1:-1, 1:-1, 1:] + padded[1:-1, 1:-1, :-1])
    return (face_x, face_y, face_z)


def diag_of(absorb, face_set):
    face_x, face_y, face_z = face_set
    return (
        absorb
        + (face_x[1:] + face_x[:-1])
        + (face_y[:, 1:] + face_y[:, :-1])
        + (face_z[:, :, 1:] + face_z[:, :, :-1])
    )


def neighbors(padded, face_set):
    face_x, face_y, face_z = face_set
    summed = face_x[1:] * padded[2:, 1:-1, 1:-1] + face_x[:-1] * padded[:-2, 1:-1, 1:-1]
    summed = (
        summed + face_y[:, 1:] * padded[1:-1, 2:, 1:-1] + face_y[:, :-1] * padded[1:-1, :-2, 1:-1]
    )
    summed = (
        summed
        + face_z[:, :, 1:] * padded[1:-1, 1:-1, 2:]
        + face_z[:, :, :-1] * padded[1:-1, 1:-1, :-2]
    )
    return summed


def checker(grid_shape):
    return (
        lax.broadcasted_iota(jnp.int32, grid_shape, 0)
        + lax.broadcasted_iota(jnp.int32, grid_shape, 1)
        + lax.broadcasted_iota(jnp.int32, grid_shape, 2)
    ) % 2


def solution_faces(field):
    return extended(field, (("gx", 0), ("gy", 1), ("gz", 2)), 1)


def to_block(boxes, source):
    box_edge = boxes.shape[1]
    picked = jnp.take(boxes, source, axis=0)
    grouped = picked.reshape(BXB, BYB, BZB, box_edge, box_edge, box_edge)
    return grouped.transpose(0, 3, 1, 4, 2, 5).reshape(
        BXB * box_edge, BYB * box_edge, BZB * box_edge
    )


def pack_sent(field_box, send_index, send_live):
    return jnp.take(field_box, send_index, axis=0) * send_live[:, None, None]


def per_device(solution_old, right_side, acoef, bcoef, corners):
    box_edge = solution_old.shape[1]
    per_dev = solution_old.shape[0]
    span_x = BXB * box_edge
    span_y = BYB * box_edge
    span_z = BZB * box_edge
    width_x = lax.axis_size("gx")
    width_y = lax.axis_size("gy")
    width_z = lax.axis_size("gz")
    myself = lax.axis_index("gy")
    table = corners.reshape(3, width_x, width_y, width_z, per_dev)
    mine_x = lax.dynamic_index_in_dim(table, lax.axis_index("gx"), 1, keepdims=False)
    mine_z = lax.dynamic_index_in_dim(mine_x, lax.axis_index("gz"), 2, keepdims=False)
    corner_x, corner_y, corner_z = (mine_z[0], mine_z[1], mine_z[2])
    owner_grid = corner_y // span_y
    inner_grid = (
        corner_x % span_x // box_edge * BYB + corner_y % span_y // box_edge
    ) * BZB + corner_z % span_z // box_edge
    my_owner = lax.dynamic_index_in_dim(owner_grid, myself, 0, keepdims=False)
    my_inner = lax.dynamic_index_in_dim(inner_grid, myself, 0, keepdims=False)
    peer_ids = jnp.arange(width_y, dtype=jnp.int32)
    slot_ids = jnp.arange(per_dev, dtype=jnp.int32)
    outgoing = (my_owner[None, :] == peer_ids[:, None]) & (peer_ids[:, None] != myself)
    send_index = jnp.sum(jnp.where(outgoing, slot_ids[None, :], 0), axis=1)
    send_live = jnp.any(outgoing, axis=1).astype(jnp.float32)
    sol_sent = pack_sent(solution_old, send_index, send_live)
    rhs_sent = pack_sent(right_side, send_index, send_live)
    absorb_sent = pack_sent(acoef, send_index, send_live)
    diffuse_sent = pack_sent(bcoef, send_index, send_live)
    sol_got, rhs_got, absorb_got, diffuse_got = (
        lax.all_to_all(sol_sent, "gy", split_axis=0, concat_axis=0, tiled=True),
        lax.all_to_all(rhs_sent, "gy", split_axis=0, concat_axis=0, tiled=True),
        lax.all_to_all(absorb_sent, "gy", split_axis=0, concat_axis=0, tiled=True),
        lax.all_to_all(diffuse_sent, "gy", split_axis=0, concat_axis=0, tiled=True),
    )
    incoming = (owner_grid == myself) & (peer_ids[:, None] != myself)
    recv_inner = jnp.sum(jnp.where(incoming, inner_grid, 0), axis=1)
    recv_live = jnp.any(incoming, axis=1)
    cand_inner = jnp.concatenate(
        [jnp.where(my_owner == myself, my_inner, -1), jnp.where(recv_live, recv_inner, -1)]
    )
    cand_ids = jnp.arange(per_dev + width_y, dtype=jnp.int32)
    source = jnp.sum(
        jnp.where(cand_inner[None, :] == slot_ids[:, None], cand_ids[None, :], 0), axis=1
    )
    solution = to_block(jnp.concatenate([solution_old, sol_got]), source)
    forcing = to_block(jnp.concatenate([right_side, rhs_got]), source)
    absorb = to_block(jnp.concatenate([acoef, absorb_got]), source)
    diffuse = to_block(jnp.concatenate([bcoef, diffuse_got]), source)
    diffuse_padded = extended(diffuse, (("gx", 0), ("gy", 1), ("gz", 2)), 1)
    face_set = face_coefs(diffuse_padded)
    diagonal = diag_of(absorb, face_set)
    parity = checker(solution.shape)
    for sweep_no in range(SWEEPS):
        for colour in (0, 1):
            padded = solution_faces(solution)
            updated = (forcing + neighbors(padded, face_set)) / diagonal
            solution = jnp.where(parity == colour, updated, solution)
    residual = forcing - (diagonal * solution - neighbors(solution_faces(solution), face_set))
    return (solution, residual)


def solution(mesh):
    in_specs = (
        P(("gx", "gy", "gz"), None, None),
        P(("gx", "gy", "gz"), None, None),
        P(("gx", "gy", "gz"), None, None),
        P(("gx", "gy", "gz"), None, None),
        P(),
    )
    out_specs = (P("gx", "gy", "gz"), P("gx", "gy", "gz"))
    return jax.shard_map(
        per_device, mesh=mesh, in_specs=in_specs, out_specs=out_specs, check_vma=False
    )
```

profile of v0, /device:TPU:29, one launch (start us, length us, event | category | flops | bytes accessed | tf_op | source)
XLA Modules:
  0.0 296.0 jit_solution(3878679453699156158)
XLA Ops:
  8.0 16.5 %all_to_all.20 = f32[4,32,1024]{2,1,0:T(8,128)S(1)} all-to-all(f32[4,32,1024]{2,1,0:T(8,128)S(1)} %get-tuple-element.57), channel_id=1, replica_groups=mesh['gx'=4,'gy'=4,'gz'=2] {'gy'}, dimensions={0} | all-to-all | bytes 1048576 | tf_op jit(solution)/shard_map/all_to_all | solution.py:114
  24.6 16.6 %all_to_all.21 = f32[4,32,1024]{2,1,0:T(8,128)S(1)} all-to-all(f32[4,32,1024]{2,1,0:T(8,128)S(1)} %get-tuple-element.58), channel_id=1, replica_groups=mesh['gx'=4,'gy'=4,'gz'=2] {'gy'}, dimensions={0} | all-to-all | bytes 1048576 | tf_op jit(solution)/shard_map/all_to_all | solution.py:111
  41.1 4.8 %all-to-all-start.3 = ((f32[4,32,1024]{2,1,0:T(8,128)}), f32[4,32,1024]{2,1,0:T(8,128)S(1)}, u32[]{:S(2)}, u32[]{:S(2)}) async-start(f32[4,32,1024]{2,1,0:T(8,128)} %get-tuple-element.59), calls=%async_computation.3 | async-start | bytes 1048576 | tf_op jit(solution)/shard_map/all_to_all | solution.py:113
  46.1 11.0 %all-to-all-done.3 = f32[4,32,1024]{2,1,0:T(8,128)S(1)} async-done(((f32[4,32,1024]{2,1,0:T(8,128)}), f32[4,32,1024]{2,1,0:T(8,128)S(1)}, u32[]{:S(2)}, u32[]{:S(2)}) %all-to-all-start.3) | async-done | bytes 524320 | tf_op jit(solution)/shard_map/all_to_all | solution.py:113
  57.1 6.2 %all-to-all-start = ((f32[4,32,1024]{2,1,0:T(8,128)}), f32[4,32,1024]{2,1,0:T(8,128)S(1)}, u32[]{:S(2)}, u32[]{:S(2)}) async-start(f32[4,32,1024]{2,1,0:T(8,128)} %get-tuple-element.60), calls=%async_computation | async-start | bytes 1048576 | tf_op jit(solution)/shard_map/all_to_all | solution.py:112
  69.3 5.2 %all-to-all-done = f32[4,32,1024]{2,1,0:T(8,128)S(1)} async-done(((f32[4,32,1024]{2,1,0:T(8,128)}), f32[4,32,1024]{2,1,0:T(8,128)S(1)}, u32[]{:S(2)}, u32[]{:S(2)}) %all-to-all-start) | async-done | bytes 524320 | tf_op jit(solution)/shard_map/all_to_all | solution.py:112
  77.0 2.3 broadcast_select_fusion.2
  79.4 2.0 reshape.67
  81.4 3.4 %copy.385 = f32[1,1,4,32,32,32]{5,2,4,1,3,0:T(4,128)S(1)} copy(f32[1,1,4,32,32,32]{5,4,3,2,1,0:T(8,128)} %reshape.67) | data formatting | bytes 1048576 | tf_op jit(solution)/shard_map/reshape | solution.py:71
  84.9 3.3 %collective-permute-start.3 = (f32[1,32,128]{2,1,0:T(8,128)S(1)}, f32[1,32,128]{2,1,0:T(8,128)S(1)}, u32[]{:S(2)}, u32[]{:S(2)}) collective-permute-start(f32[1,32,128]{2,1,0:T(8,128)S(1)} %slice.333), channel_id=1, source_target_pairs={{0,8},{8,16},{16,24},{1,9},{9,17},{17,25},{2,10},{10,18},{18,26},{... | collective-permute-start | bytes 49160 | tf_op jit(solution)/shard_map/ppermute | solution.py:17
  88.2 2.9 reshape.65
  93.7 3.4 %copy.310 = f32[1,32,1,32,4,32]{5,4,3,1,2,0:T(4,128)S(1)} copy(f32[1,32,1,32,4,32]{5,3,1,4,2,0:T(8,128)} %bitcast.36) | data formatting | bytes 1048576 | tf_op jit(solution)/shard_map/transpose | solution.py:72
  97.1 2.0 reshape.63
  99.1 4.7 %copy.386 = f32[1,1,4,32,32,32]{5,2,4,3,1,0:T(4,128)} copy(f32[1,1,4,32,32,32]{5,4,3,2,1,0:T(8,128)} %reshape.63) | data formatting | bytes 1048576 | tf_op jit(solution)/shard_map/reshape | solution.py:71
  103.9 2.4 reshape.64
  106.4 3.1 %collective-permute-start.2 = (f32[1,32,128]{2,1,0:T(8,128)S(1)}, f32[1,32,128]{2,1,0:T(8,128)S(1)}, u32[]{:S(2)}, u32[]{:S(2)}) collective-permute-start(f32[1,32,128]{2,1,0:T(8,128)S(1)} %slice.329), channel_id=1, source_target_pairs={{8,0},{16,8},{24,16},{9,1},{17,9},{25,17},{10,2},{18,10},{26,18},{... | collective-permute-start | bytes 49160 | tf_op jit(solution)/shard_map/ppermute | solution.py:20
  109.5 2.0 reshape.69
  111.5 4.7 %copy.384 = f32[1,1,4,32,32,32]{5,2,4,3,1,0:T(4,128)} copy(f32[1,1,4,32,32,32]{5,4,3,2,1,0:T(8,128)} %reshape.69) | data formatting | bytes 1048576 | tf_op jit(solution)/shard_map/reshape | solution.py:71
  116.2 2.4 reshape.70
  118.8 2.2 collective-permute-start.1
  122.9 4.3 %collective-permute-start = (f32[1,32,128]{2,1,0:T(8,128)S(1)}, f32[1,32,128]{2,1,0:T(8,128)S(1)}, u32[]{:S(2)}, u32[]{:S(2)}) collective-permute-start(f32[1,32,128]{2,1,0:T(8,128)S(1)} %slice.324), channel_id=1, source_target_pairs={{8,0},{16,8},{24,16},{9,1},{17,9},{25,17},{10,2},{18,10},{26,18},{... | collective-permute-start | bytes 49160 | tf_op jit(solution)/shard_map/ppermute | solution.py:20
  132.7 4.0 %collective-permute-start.4 = (f32[34,1,128]{2,0,1:T(8,128)S(1)}, f32[34,1,128]{2,0,1:T(8,128)S(1)}, u32[]{:S(2)}, u32[]{:S(2)}) collective-permute-start(f32[34,1,128]{2,0,1:T(8,128)S(1)} %copy.379), channel_id=1, source_target_pairs={{2,0},{4,2},{6,4},{3,1},{5,3},{7,5},{10,8},{12,10},{14,12},{11,9},... | collective-permute-start | bytes 52232 | tf_op jit(solution)/shard_map/ppermute | solution.py:20
  139.6 2.2 collective-permute-done.5
  147.4 6.1 %collective-permute-start.8 = (f32[34,34,1]{1,0,2:T(8,128)S(1)}, f32[34,34,1]{1,0,2:T(8,128)S(1)}, u32[]{:S(2)}, u32[]{:S(2)}) collective-permute-start(f32[34,34,1]{1,0,2:T(8,128)S(1)} %copy.324), channel_id=1, source_target_pairs={{1,0},{3,2},{5,4},{7,6},{9,8},{11,10},{13,12},{15,14},{17,16},{19,... | collective-permute-start | bytes 13880 | tf_op jit(solution)/shard_map/ppermute | solution.py:20
  157.8 3.0 %collective-permute-start.10 = (f32[34,34,1]{1,0,2:T(8,128)S(1)}, f32[34,34,1]{1,0,2:T(8,128)S(1)}, u32[]{:S(2)}, u32[]{:S(2)}) collective-permute-start(f32[34,34,1]{1,0,2:T(8,128)S(1)} %copy.330), channel_id=1, source_target_pairs={{1,0},{3,2},{5,4},{7,6},{9,8},{11,10},{13,12},{15,14},{17,16},{19,... | collective-permute-start | bytes 13880 | tf_op jit(solution)/shard_map/ppermute | solution.py:20
  163.3 2.0 fusion.1
  167.7 3.3 %fusion.65 = f32[32,32,128]{2,1,0:T(8,128)S(1)} fusion(f32[32,32,128]{2,1,0:T(8,128)} %reshape.68, f32[32,32,128]{2,1,0:T(8,128)S(1)} %reshape.64, f32[34,34,1]{2,1,0:T(8,128)} %copy.333, f32[34,1,128]{2,1,0:T(1,128)S(1)} %copy.319, f32[34,32,128]{2,1,0:T(8,128)} %copy-done.6, f32[34,1,128]{2,1,0:T(1,128)S(1)} %copy.321, f32[34,34,1]{2,1,0:T(8,128)} %copy.331, ...), kind=kLoop, calls=%fused_computation.171 | loop fusion | flops 5767168 | bytes 5876768 | tf_op jit(solution)/shard_map/jit(_where)/select_n | solution.py:138
  173.0 3.4 %collective-permute-start.13 = (f32[1,32,128]{2,1,0:T(8,128)S(1)}, f32[1,32,128]{2,1,0:T(8,128)S(1)}, u32[]{:S(2)}, u32[]{:S(2)}) collective-permute-start(f32[1,32,128]{2,1,0:T(8,128)S(1)} %get-tuple-element.52), channel_id=1, source_target_pairs={{0,8},{8,16},{16,24},{1,9},{9,17},{17,25},{2,10},{10,18},{18,26},{... | collective-permute-start | bytes 49160 | tf_op jit(solution)/shard_map/ppermute | solution.py:17
  176.4 2.2 collective-permute-done.13
  178.6 3.5 %collective-permute-start.14 = (f32[34,1,128]{2,0,1:T(8,128)S(1)}, f32[34,1,128]{2,0,1:T(8,128)S(1)}, u32[]{:S(2)}, u32[]{:S(2)}) collective-permute-start(f32[34,1,128]{2,0,1:T(8,128)S(1)} %copy.335), channel_id=1, source_target_pairs={{2,0},{4,2},{6,4},{3,1},{5,3},{7,5},{10,8},{12,10},{14,12},{11,9},... | collective-permute-start | bytes 52232 | tf_op jit(solution)/shard_map/ppermute | solution.py:20
  183.4 3.5 %collective-permute-done.15 = f32[34,1,128]{2,0,1:T(8,128)S(1)} collective-permute-done((f32[34,1,128]{2,0,1:T(8,128)S(1)}, f32[34,1,128]{2,0,1:T(8,128)S(1)}, u32[]{:S(2)}, u32[]{:S(2)}) %collective-permute-start.15) | collective-permute-done | bytes 17440 | tf_op jit(solution)/shard_map/ppermute | solution.py:17
  192.6 3.4 %collective-permute-start.16 = (f32[34,34,1]{1,0,2:T(8,128)S(1)}, f32[34,34,1]{1,0,2:T(8,128)S(1)}, u32[]{:S(2)}, u32[]{:S(2)}) collective-permute-start(f32[34,34,1]{1,0,2:T(8,128)S(1)} %copy.341), channel_id=1, source_target_pairs={{1,0},{3,2},{5,4},{7,6},{9,8},{11,10},{13,12},{15,14},{17,16},{19,... | collective-permute-start | bytes 13880 | tf_op jit(solution)/shard_map/ppermute | solution.py:20
  198.4 4.2 %fusion.51 = f32[32,32,128]{2,1,0:T(8,128)S(1)} fusion(f32[32,32,128]{2,1,0:T(8,128)} %copy-done.3, f32[32,32,128]{2,1,0:T(8,128)S(1)} %reshape.64, f32[34,34,1]{2,1,0:T(8,128)} %copy.344, f32[34,1,128]{2,1,0:T(1,128)S(1)} %copy.336, f32[34,1,128]{2,1,0:T(1,128)S(1)} %copy.338, f32[1,32,128]{2,1,0:T(8,128)S(1)} %collective-permute-done.12, ...), kind=kLoop, calls=%fused_computation.139 | loop fusion | flops 6815744 | bytes 5319712 | tf_op jit(solution)/shard_map/jit(_where)/select_n | solution.py:138
  204.6 3.4 %collective-permute-start.19 = (f32[1,32,128]{2,1,0:T(8,128)S(1)}, f32[1,32,128]{2,1,0:T(8,128)S(1)}, u32[]{:S(2)}, u32[]{:S(2)}) collective-permute-start(f32[1,32,128]{2,1,0:T(8,128)S(1)} %get-tuple-element.50), channel_id=1, source_target_pairs={{0,8},{8,16},{16,24},{1,9},{9,17},{17,25},{2,10},{10,18},{18,26},{... | collective-permute-start | bytes 49160 | tf_op jit(solution)/shard_map/ppermute | solution.py:17
  207.9 2.0 collective-permute-done.19
  210.0 3.6 %collective-permute-start.20 = (f32[34,1,128]{2,0,1:T(8,128)S(1)}, f32[34,1,128]{2,0,1:T(8,128)S(1)}, u32[]{:S(2)}, u32[]{:S(2)}) collective-permute-start(f32[34,1,128]{2,0,1:T(8,128)S(1)} %copy.345), channel_id=1, source_target_pairs={{2,0},{4,2},{6,4},{3,1},{5,3},{7,5},{10,8},{12,10},{14,12},{11,9},... | collective-permute-start | bytes 52232 | tf_op jit(solution)/shard_map/ppermute | solution.py:20
  215.0 3.2 %collective-permute-done.21 = f32[34,1,128]{2,0,1:T(8,128)S(1)} collective-permute-done((f32[34,1,128]{2,0,1:T(8,128)S(1)}, f32[34,1,128]{2,0,1:T(8,128)S(1)}, u32[]{:S(2)}, u32[]{:S(2)}) %collective-permute-start.21) | collective-permute-done | bytes 17440 | tf_op jit(solution)/shard_map/ppermute | solution.py:17
  223.8 4.4 %collective-permute-start.22 = (f32[34,34,1]{1,0,2:T(8,128)S(1)}, f32[34,34,1]{1,0,2:T(8,128)S(1)}, u32[]{:S(2)}, u32[]{:S(2)}) collective-permute-start(f32[34,34,1]{1,0,2:T(8,128)S(1)} %copy.351), channel_id=1, source_target_pairs={{1,0},{3,2},{5,4},{7,6},{9,8},{11,10},{13,12},{15,14},{17,16},{19,... | collective-permute-start | bytes 13880 | tf_op jit(solution)/shard_map/ppermute | solution.py:20
  230.7 4.2 %fusion.37 = f32[32,32,128]{2,1,0:T(8,128)S(1)} fusion(f32[32,32,128]{2,1,0:T(8,128)} %copy-done.1, f32[32,32,128]{2,1,0:T(8,128)S(1)} %reshape.64, f32[34,34,1]{2,1,0:T(8,128)} %copy.354, f32[34,1,128]{2,1,0:T(1,128)S(1)} %copy.346, f32[34,1,128]{2,1,0:T(1,128)S(1)} %copy.348, f32[1,32,128]{2,1,0:T(8,128)S(1)} %collective-permute-done.18, ...), kind=kLoop, calls=%fused_computation.107 | loop fusion | flops 6815744 | bytes 5319712 | tf_op jit(solution)/shard_map/jit(_where)/select_n | solution.py:138
  236.8 3.4 %collective-permute-start.25 = (f32[1,32,128]{2,1,0:T(8,128)S(1)}, f32[1,32,128]{2,1,0:T(8,128)S(1)}, u32[]{:S(2)}, u32[]{:S(2)}) collective-permute-start(f32[1,32,128]{2,1,0:T(8,128)S(1)} %get-tuple-element.48), channel_id=1, source_target_pairs={{0,8},{8,16},{16,24},{1,9},{9,17},{17,25},{2,10},{10,18},{18,26},{... | collective-permute-start | bytes 49160 | tf_op jit(solution)/shard_map/ppermute | solution.py:17
  240.2 2.0 collective-permute-done.25
  245.2 3.2 %collective-permute-done.27 = f32[34,1,128]{2,0,1:T(8,128)S(1)} collective-permute-done((f32[34,1,128]{2,0,1:T(8,128)S(1)}, f32[34,1,128]{2,0,1:T(8,128)S(1)}, u32[]{:S(2)}, u32[]{:S(2)}) %collective-permute-start.27) | collective-permute-done | bytes 17440 | tf_op jit(solution)/shard_map/ppermute | solution.py:17
  254.1 4.4 %collective-permute-start.28 = (f32[34,34,1]{1,0,2:T(8,128)S(1)}, f32[34,34,1]{1,0,2:T(8,128)S(1)}, u32[]{:S(2)}, u32[]{:S(2)}) collective-permute-start(f32[34,34,1]{1,0,2:T(8,128)S(1)} %copy.361), channel_id=1, source_target_pairs={{1,0},{3,2},{5,4},{7,6},{9,8},{11,10},{13,12},{15,14},{17,16},{19,... | collective-permute-start | bytes 13880 | tf_op jit(solution)/shard_map/ppermute | solution.py:20
  261.0 4.2 %fusion.23 = f32[32,32,128]{2,1,0:T(8,128)S(1)} fusion(f32[32,32,128]{2,1,0:T(8,128)} %copy-done.2, f32[32,32,128]{2,1,0:T(8,128)S(1)} %reshape.64, f32[34,34,1]{2,1,0:T(8,128)} %copy.364, f32[34,1,128]{2,1,0:T(1,128)S(1)} %copy.356, f32[34,1,128]{2,1,0:T(1,128)S(1)} %copy.358, f32[1,32,128]{2,1,0:T(8,128)S(1)} %collective-permute-done.24, ...), kind=kLoop, calls=%fused_computation.75 | loop fusion | flops 6815744 | bytes 5319712 | tf_op jit(solution)/shard_map/jit(_where)/select_n | solution.py:138
  267.1 3.4 %collective-permute-start.31 = (f32[1,32,128]{2,1,0:T(8,128)S(1)}, f32[1,32,128]{2,1,0:T(8,128)S(1)}, u32[]{:S(2)}, u32[]{:S(2)}) collective-permute-start(f32[1,32,128]{2,1,0:T(8,128)S(1)} %get-tuple-element.46), channel_id=1, source_target_pairs={{0,8},{8,16},{16,24},{1,9},{9,17},{17,25},{2,10},{10,18},{18,26},{... | collective-permute-start | bytes 49160 | tf_op jit(solution)/shard_map/ppermute | solution.py:17
  275.5 3.2 %collective-permute-done.33 = f32[34,1,128]{2,0,1:T(8,128)S(1)} collective-permute-done((f32[34,1,128]{2,0,1:T(8,128)S(1)}, f32[34,1,128]{2,0,1:T(8,128)S(1)}, u32[]{:S(2)}, u32[]{:S(2)}) %collective-permute-start.33) | collective-permute-done | bytes 17440 | tf_op jit(solution)/shard_map/ppermute | solution.py:17
  284.4 4.4 %collective-permute-start.34 = (f32[34,34,1]{1,0,2:T(8,128)S(1)}, f32[34,34,1]{1,0,2:T(8,128)S(1)}, u32[]{:S(2)}, u32[]{:S(2)}) collective-permute-start(f32[34,34,1]{1,0,2:T(8,128)S(1)} %copy.371), channel_id=1, source_target_pairs={{1,0},{3,2},{5,4},{7,6},{9,8},{11,10},{13,12},{15,14},{17,16},{19,... | collective-permute-start | bytes 13880 | tf_op jit(solution)/shard_map/ppermute | solution.py:20
  291.2 4.8 %fusion.9 = f32[32,32,128]{2,1,0:T(8,128)} fusion(f32[32,32,128]{2,1,0:T(8,128)S(1)} %reshape.64, f32[34,34,1]{2,1,0:T(8,128)} %copy.374, f32[34,1,128]{2,1,0:T(1,128)S(1)} %copy.366, f32[34,1,128]{2,1,0:T(1,128)S(1)} %copy.368, f32[1,32,128]{2,1,0:T(8,128)S(1)} %collective-permute-done.30, f32[32,32,128]{2,1,0:T(8,128)} %copy-done, ...), kind=kLoop, calls=%fused_computation.43 | loop fusion | flops 4980736 | bytes 5319712 | tf_op jit(solution)/shard_map/sub | solution.py:139
  (183 shorter events, 94.2 us)
Async XLA Ops:
  0.6 5.0 %copy-start.7 = (f32[4,32,1024]{2,1,0:T(8,128)S(1)}, f32[4,32,1024]{2,1,0:T(8,128)}, u32[]{:S(2)}) copy-start(f32[4,32,1024]{2,1,0:T(8,128)} %param.11) | copy-start | bytes 1572868
  0.6 5.6 %copy-start.8 = (f32[4,32,1024]{2,1,0:T(8,128)S(1)}, f32[4,32,1024]{2,1,0:T(8,128)}, u32[]{:S(2)}) copy-start(f32[4,32,1024]{2,1,0:T(8,128)} %param.10) | copy-start | bytes 1572868
  41.1 16.0 %all-to-all-start.3 = ((f32[4,32,1024]{2,1,0:T(8,128)}), f32[4,32,1024]{2,1,0:T(8,128)S(1)}, u32[]{:S(2)}, u32[]{:S(2)}) async-start(f32[4,32,1024]{2,1,0:T(8,128)} %get-tuple-element.59), calls=%async_computation.3 | async-start | bytes 1048576 | tf_op jit(solution)/shard_map/all_to_all | solution.py:113
  57.1 17.4 %all-to-all-start = ((f32[4,32,1024]{2,1,0:T(8,128)}), f32[4,32,1024]{2,1,0:T(8,128)S(1)}, u32[]{:S(2)}, u32[]{:S(2)}) async-start(f32[4,32,1024]{2,1,0:T(8,128)} %get-tuple-element.60), calls=%async_computation | async-start | bytes 1048576 | tf_op jit(solution)/shard_map/all_to_all | solution.py:112
  84.9 42.3 %collective-permute-start.3 = (f32[1,32,128]{2,1,0:T(8,128)S(1)}, f32[1,32,128]{2,1,0:T(8,128)S(1)}, u32[]{:S(2)}, u32[]{:S(2)}) collective-permute-start(f32[1,32,128]{2,1,0:T(8,128)S(1)} %slice.333), channel_id=1, source_target_pairs={{0,8},{8,16},{16,24},{1,9},{9,17},{17,25},{2,10},{10,18},{18,26},{... | collective-permute-start | bytes 49160 | tf_op jit(solution)/shard_map/ppermute | solution.py:17
  106.4 21.9 %collective-permute-start.2 = (f32[1,32,128]{2,1,0:T(8,128)S(1)}, f32[1,32,128]{2,1,0:T(8,128)S(1)}, u32[]{:S(2)}, u32[]{:S(2)}) collective-permute-start(f32[1,32,128]{2,1,0:T(8,128)S(1)} %slice.329), channel_id=1, source_target_pairs={{8,0},{16,8},{24,16},{9,1},{17,9},{25,17},{10,2},{18,10},{26,18},{... | collective-permute-start | bytes 49160 | tf_op jit(solution)/shard_map/ppermute | solution.py:20
  118.8 12.7 %collective-permute-start.1 = (f32[1,32,128]{2,1,0:T(8,128)S(1)}, f32[1,32,128]{2,1,0:T(8,128)S(1)}, u32[]{:S(2)}, u32[]{:S(2)}) collective-permute-start(f32[1,32,128]{2,1,0:T(8,128)S(1)} %slice.326), channel_id=1, source_target_pairs={{0,8},{8,16},{16,24},{1,9},{9,17},{17,25},{2,10},{10,18},{18,26},{... | collective-permute-start | bytes 49160 | tf_op jit(solution)/shard_map/ppermute | solution.py:17
  122.7 15.3 %copy-start.5 = (f32[32,32,128]{2,1,0:T(8,128)S(1)}, f32[32,32,128]{2,1,0:T(8,128)}, u32[]{:S(2)}) copy-start(f32[32,32,128]{2,1,0:T(8,128)} %reshape.66) | copy-start | bytes 1572868
  122.9 9.7 %collective-permute-start = (f32[1,32,128]{2,1,0:T(8,128)S(1)}, f32[1,32,128]{2,1,0:T(8,128)S(1)}, u32[]{:S(2)}, u32[]{:S(2)}) collective-permute-start(f32[1,32,128]{2,1,0:T(8,128)S(1)} %slice.324), channel_id=1, source_target_pairs={{8,0},{16,8},{24,16},{9,1},{17,9},{25,17},{10,2},{18,10},{26,18},{... | collective-permute-start | bytes 49160 | tf_op jit(solution)/shard_map/ppermute | solution.py:20
  128.3 9.8 %copy-start.6 = (f32[34,32,128]{2,1,0:T(8,128)}, f32[34,32,128]{2,1,0:T(8,128)S(1)}, u32[]{:S(2)}) copy-start(f32[34,32,128]{2,1,0:T(8,128)S(1)} %constant_dynamic-update-slice_fusion.3) | copy-start | bytes 1671172
  128.4 9.7 %collective-permute-start.6 = (f32[34,1,128]{2,0,1:T(8,128)S(1)}, f32[34,1,128]{2,0,1:T(8,128)S(1)}, u32[]{:S(2)}, u32[]{:S(2)}) collective-permute-start(f32[34,1,128]{2,0,1:T(8,128)S(1)} %copy.318), channel_id=1, source_target_pairs={{2,0},{4,2},{6,4},{3,1},{5,3},{7,5},{10,8},{12,10},{14,12},{11,9},... | collective-permute-start | bytes 52232 | tf_op jit(solution)/shard_map/ppermute | solution.py:20
  130.2 7.9 %collective-permute-start.7 = (f32[34,1,128]{2,0,1:T(8,128)S(1)}, f32[34,1,128]{2,0,1:T(8,128)S(1)}, u32[]{:S(2)}, u32[]{:S(2)}) collective-permute-start(f32[34,1,128]{2,0,1:T(8,128)S(1)} %copy.320), channel_id=1, source_target_pairs={{0,2},{2,4},{4,6},{1,3},{3,5},{5,7},{8,10},{10,12},{12,14},{9,11},... | collective-permute-start | bytes 52232 | tf_op jit(solution)/shard_map/ppermute | solution.py:17
  132.6 20.9 %copy-start.4 = (f32[34,32,128]{2,1,0:T(8,128)}, f32[34,32,128]{2,1,0:T(8,128)S(1)}, u32[]{:S(2)}) copy-start(f32[34,32,128]{2,1,0:T(8,128)S(1)} %constant_dynamic-update-slice_fusion) | copy-start | bytes 1671172
  132.7 6.9 %collective-permute-start.4 = (f32[34,1,128]{2,0,1:T(8,128)S(1)}, f32[34,1,128]{2,0,1:T(8,128)S(1)}, u32[]{:S(2)}, u32[]{:S(2)}) collective-permute-start(f32[34,1,128]{2,0,1:T(8,128)S(1)} %copy.379), channel_id=1, source_target_pairs={{2,0},{4,2},{6,4},{3,1},{5,3},{7,5},{10,8},{12,10},{14,12},{11,9},... | collective-permute-start | bytes 52232 | tf_op jit(solution)/shard_map/ppermute | solution.py:20
  136.7 5.0 %collective-permute-start.5 = (f32[34,1,128]{2,0,1:T(8,128)S(1)}, f32[34,1,128]{2,0,1:T(8,128)S(1)}, u32[]{:S(2)}, u32[]{:S(2)}) collective-permute-start(f32[34,1,128]{2,0,1:T(8,128)S(1)} %copy.380), channel_id=1, source_target_pairs={{0,2},{2,4},{4,6},{1,3},{3,5},{5,7},{8,10},{10,12},{12,14},{9,11},... | collective-permute-start | bytes 52232 | tf_op jit(solution)/shard_map/ppermute | solution.py:17
  144.6 16.3 %collective-permute-start.9 = (f32[34,34,1]{1,0,2:T(8,128)S(1)}, f32[34,34,1]{1,0,2:T(8,128)S(1)}, u32[]{:S(2)}, u32[]{:S(2)}) collective-permute-start(f32[34,34,1]{1,0,2:T(8,128)S(1)} %copy.326), channel_id=1, source_target_pairs={{0,1},{2,3},{4,5},{6,7},{8,9},{10,11},{12,13},{14,15},{16,17},{18,... | collective-permute-start | bytes 13880 | tf_op jit(solution)/shard_map/ppermute | solution.py:17
  147.4 14.7 %collective-permute-start.8 = (f32[34,34,1]{1,0,2:T(8,128)S(1)}, f32[34,34,1]{1,0,2:T(8,128)S(1)}, u32[]{:S(2)}, u32[]{:S(2)}) collective-permute-start(f32[34,34,1]{1,0,2:T(8,128)S(1)} %copy.324), channel_id=1, source_target_pairs={{1,0},{3,2},{5,4},{7,6},{9,8},{11,10},{13,12},{15,14},{17,16},{19,... | collective-permute-start | bytes 13880 | tf_op jit(solution)/shard_map/ppermute | solution.py:20
  155.0 10.2 %collective-permute-start.11 = (f32[34,34,1]{1,0,2:T(8,128)S(1)}, f32[34,34,1]{1,0,2:T(8,128)S(1)}, u32[]{:S(2)}, u32[]{:S(2)}) collective-permute-start(f32[34,34,1]{1,0,2:T(8,128)S(1)} %copy.332), channel_id=1, source_target_pairs={{0,1},{2,3},{4,5},{6,7},{8,9},{10,11},{12,13},{14,15},{16,17},{18,... | collective-permute-start | bytes 13880 | tf_op jit(solution)/shard_map/ppermute | solution.py:17
  157.8 8.7 %collective-permute-start.10 = (f32[34,34,1]{1,0,2:T(8,128)S(1)}, f32[34,34,1]{1,0,2:T(8,128)S(1)}, u32[]{:S(2)}, u32[]{:S(2)}) collective-permute-start(f32[34,34,1]{1,0,2:T(8,128)S(1)} %copy.330), channel_id=1, source_target_pairs={{1,0},{3,2},{5,4},{7,6},{9,8},{11,10},{13,12},{15,14},{17,16},{19,... | collective-permute-start | bytes 13880 | tf_op jit(solution)/shard_map/ppermute | solution.py:20
  171.1 17.3 %copy-start.3 = (f32[32,32,128]{2,1,0:T(8,128)}, f32[32,32,128]{2,1,0:T(8,128)S(1)}, u32[]{:S(2)}) copy-start(f32[32,32,128]{2,1,0:T(8,128)S(1)} %fusion.65) | copy-start | bytes 1572868
  171.1 5.3 %collective-permute-start.12 = (f32[1,32,128]{2,1,0:T(8,128)S(1)}, f32[1,32,128]{2,1,0:T(8,128)S(1)}, u32[]{:S(2)}, u32[]{:S(2)}) collective-permute-start(f32[1,32,128]{2,1,0:T(8,128)S(1)} %get-tuple-element.53), channel_id=1, source_target_pairs={{8,0},{16,8},{24,16},{9,1},{17,9},{25,17},{10,2},{18,10},{26,18},{... | collective-permute-start | bytes 49160 | tf_op jit(solution)/shard_map/ppermute | solution.py:20
  173.0 5.5 %collective-permute-start.13 = (f32[1,32,128]{2,1,0:T(8,128)S(1)}, f32[1,32,128]{2,1,0:T(8,128)S(1)}, u32[]{:S(2)}, u32[]{:S(2)}) collective-permute-start(f32[1,32,128]{2,1,0:T(8,128)S(1)} %get-tuple-element.52), channel_id=1, source_target_pairs={{0,8},{8,16},{16,24},{1,9},{9,17},{17,25},{2,10},{10,18},{18,26},{... | collective-permute-start | bytes 49160 | tf_op jit(solution)/shard_map/ppermute | solution.py:17
  178.6 4.8 %collective-permute-start.14 = (f32[34,1,128]{2,0,1:T(8,128)S(1)}, f32[34,1,128]{2,0,1:T(8,128)S(1)}, u32[]{:S(2)}, u32[]{:S(2)}) collective-permute-start(f32[34,1,128]{2,0,1:T(8,128)S(1)} %copy.335), channel_id=1, source_target_pairs={{2,0},{4,2},{6,4},{3,1},{5,3},{7,5},{10,8},{12,10},{14,12},{11,9},... | collective-permute-start | bytes 52232 | tf_op jit(solution)/shard_map/ppermute | solution.py:20
  182.1 4.8 %collective-permute-start.15 = (f32[34,1,128]{2,0,1:T(8,128)S(1)}, f32[34,1,128]{2,0,1:T(8,128)S(1)}, u32[]{:S(2)}, u32[]{:S(2)}) collective-permute-start(f32[34,1,128]{2,0,1:T(8,128)S(1)} %copy.337), channel_id=1, source_target_pairs={{0,2},{2,4},{4,6},{1,3},{3,5},{5,7},{8,10},{10,12},{12,14},{9,11},... | collective-permute-start | bytes 52232 | tf_op jit(solution)/shard_map/ppermute | solution.py:17
  189.8 6.2 %collective-permute-start.17 = (f32[34,34,1]{1,0,2:T(8,128)S(1)}, f32[34,34,1]{1,0,2:T(8,128)S(1)}, u32[]{:S(2)}, u32[]{:S(2)}) collective-permute-start(f32[34,34,1]{1,0,2:T(8,128)S(1)} %copy.343), channel_id=1, source_target_pairs={{0,1},{2,3},{4,5},{6,7},{8,9},{10,11},{12,13},{14,15},{16,17},{18,... | collective-permute-start | bytes 13880 | tf_op jit(solution)/shard_map/ppermute | solution.py:17
  192.6 4.7 %collective-permute-start.16 = (f32[34,34,1]{1,0,2:T(8,128)S(1)}, f32[34,34,1]{1,0,2:T(8,128)S(1)}, u32[]{:S(2)}, u32[]{:S(2)}) collective-permute-start(f32[34,34,1]{1,0,2:T(8,128)S(1)} %copy.341), channel_id=1, source_target_pairs={{1,0},{3,2},{5,4},{7,6},{9,8},{11,10},{13,12},{15,14},{17,16},{19,... | collective-permute-start | bytes 13880 | tf_op jit(solution)/shard_map/ppermute | solution.py:20
  202.6 15.6 %copy-start.1 = (f32[32,32,128]{2,1,0:T(8,128)}, f32[32,32,128]{2,1,0:T(8,128)S(1)}, u32[]{:S(2)}) copy-start(f32[32,32,128]{2,1,0:T(8,128)S(1)} %fusion.51) | copy-start | bytes 1572868
  202.6 5.3 %collective-permute-start.18 = (f32[1,32,128]{2,1,0:T(8,128)S(1)}, f32[1,32,128]{2,1,0:T(8,128)S(1)}, u32[]{:S(2)}, u32[]{:S(2)}) collective-permute-start(f32[1,32,128]{2,1,0:T(8,128)S(1)} %get-tuple-element.51), channel_id=1, source_target_pairs={{8,0},{16,8},{24,16},{9,1},{17,9},{25,17},{10,2},{18,10},{26,18},{... | collective-permute-start | bytes 49160 | tf_op jit(solution)/shard_map/ppermute | solution.py:20
  204.6 5.4 %collective-permute-start.19 = (f32[1,32,128]{2,1,0:T(8,128)S(1)}, f32[1,32,128]{2,1,0:T(8,128)S(1)}, u32[]{:S(2)}, u32[]{:S(2)}) collective-permute-start(f32[1,32,128]{2,1,0:T(8,128)S(1)} %get-tuple-element.50), channel_id=1, source_target_pairs={{0,8},{8,16},{16,24},{1,9},{9,17},{17,25},{2,10},{10,18},{18,26},{... | collective-permute-start | bytes 49160 | tf_op jit(solution)/shard_map/ppermute | solution.py:17
  210.0 5.0 %collective-permute-start.20 = (f32[34,1,128]{2,0,1:T(8,128)S(1)}, f32[34,1,128]{2,0,1:T(8,128)S(1)}, u32[]{:S(2)}, u32[]{:S(2)}) collective-permute-start(f32[34,1,128]{2,0,1:T(8,128)S(1)} %copy.345), channel_id=1, source_target_pairs={{2,0},{4,2},{6,4},{3,1},{5,3},{7,5},{10,8},{12,10},{14,12},{11,9},... | collective-permute-start | bytes 52232 | tf_op jit(solution)/shard_map/ppermute | solution.py:20
  213.6 4.5 %collective-permute-start.21 = (f32[34,1,128]{2,0,1:T(8,128)S(1)}, f32[34,1,128]{2,0,1:T(8,128)S(1)}, u32[]{:S(2)}, u32[]{:S(2)}) collective-permute-start(f32[34,1,128]{2,0,1:T(8,128)S(1)} %copy.347), channel_id=1, source_target_pairs={{0,2},{2,4},{4,6},{1,3},{3,5},{5,7},{8,10},{10,12},{12,14},{9,11},... | collective-permute-start | bytes 52232 | tf_op jit(solution)/shard_map/ppermute | solution.py:17
  221.1 7.2 %collective-permute-start.23 = (f32[34,34,1]{1,0,2:T(8,128)S(1)}, f32[34,34,1]{1,0,2:T(8,128)S(1)}, u32[]{:S(2)}, u32[]{:S(2)}) collective-permute-start(f32[34,34,1]{1,0,2:T(8,128)S(1)} %copy.353), channel_id=1, source_target_pairs={{0,1},{2,3},{4,5},{6,7},{8,9},{10,11},{12,13},{14,15},{16,17},{18,... | collective-permute-start | bytes 13880 | tf_op jit(solution)/shard_map/ppermute | solution.py:17
  223.8 5.7 %collective-permute-start.22 = (f32[34,34,1]{1,0,2:T(8,128)S(1)}, f32[34,34,1]{1,0,2:T(8,128)S(1)}, u32[]{:S(2)}, u32[]{:S(2)}) collective-permute-start(f32[34,34,1]{1,0,2:T(8,128)S(1)} %copy.351), channel_id=1, source_target_pairs={{1,0},{3,2},{5,4},{7,6},{9,8},{11,10},{13,12},{15,14},{17,16},{19,... | collective-permute-start | bytes 13880 | tf_op jit(solution)/shard_map/ppermute | solution.py:20
  234.9 13.6 %copy-start.2 = (f32[32,32,128]{2,1,0:T(8,128)}, f32[32,32,128]{2,1,0:T(8,128)S(1)}, u32[]{:S(2)}) copy-start(f32[32,32,128]{2,1,0:T(8,128)S(1)} %fusion.37) | copy-start | bytes 1572868
  234.9 5.3 %collective-permute-start.24 = (f32[1,32,128]{2,1,0:T(8,128)S(1)}, f32[1,32,128]{2,1,0:T(8,128)S(1)}, u32[]{:S(2)}, u32[]{:S(2)}) collective-permute-start(f32[1,32,128]{2,1,0:T(8,128)S(1)} %get-tuple-element.49), channel_id=1, source_target_pairs={{8,0},{16,8},{24,16},{9,1},{17,9},{25,17},{10,2},{18,10},{26,18},{... | collective-permute-start | bytes 49160 | tf_op jit(solution)/shard_map/ppermute | solution.py:20
  236.8 5.4 %collective-permute-start.25 = (f32[1,32,128]{2,1,0:T(8,128)S(1)}, f32[1,32,128]{2,1,0:T(8,128)S(1)}, u32[]{:S(2)}, u32[]{:S(2)}) collective-permute-start(f32[1,32,128]{2,1,0:T(8,128)S(1)} %get-tuple-element.48), channel_id=1, source_target_pairs={{0,8},{8,16},{16,24},{1,9},{9,17},{17,25},{2,10},{10,18},{18,26},{... | collective-permute-start | bytes 49160 | tf_op jit(solution)/shard_map/ppermute | solution.py:17
  242.2 3.0 %collective-permute-start.26 = (f32[34,1,128]{2,0,1:T(8,128)S(1)}, f32[34,1,128]{2,0,1:T(8,128)S(1)}, u32[]{:S(2)}, u32[]{:S(2)}) collective-permute-start(f32[34,1,128]{2,0,1:T(8,128)S(1)} %copy.355), channel_id=1, source_target_pairs={{2,0},{4,2},{6,4},{3,1},{5,3},{7,5},{10,8},{12,10},{14,12},{11,9},... | collective-permute-start | bytes 52232 | tf_op jit(solution)/shard_map/ppermute | solution.py:20
  243.9 4.5 %collective-permute-start.27 = (f32[34,1,128]{2,0,1:T(8,128)S(1)}, f32[34,1,128]{2,0,1:T(8,128)S(1)}, u32[]{:S(2)}, u32[]{:S(2)}) collective-permute-start(f32[34,1,128]{2,0,1:T(8,128)S(1)} %copy.357), channel_id=1, source_target_pairs={{0,2},{2,4},{4,6},{1,3},{3,5},{5,7},{8,10},{10,12},{12,14},{9,11},... | collective-permute-start | bytes 52232 | tf_op jit(solution)/shard_map/ppermute | solution.py:17
  251.3 7.2 %collective-permute-start.29 = (f32[34,34,1]{1,0,2:T(8,128)S(1)}, f32[34,34,1]{1,0,2:T(8,128)S(1)}, u32[]{:S(2)}, u32[]{:S(2)}) collective-permute-start(f32[34,34,1]{1,0,2:T(8,128)S(1)} %copy.363), channel_id=1, source_target_pairs={{0,1},{2,3},{4,5},{6,7},{8,9},{10,11},{12,13},{14,15},{16,17},{18,... | collective-permute-start | bytes 13880 | tf_op jit(solution)/shard_map/ppermute | solution.py:17
  254.1 5.7 %collective-permute-start.28 = (f32[34,34,1]{1,0,2:T(8,128)S(1)}, f32[34,34,1]{1,0,2:T(8,128)S(1)}, u32[]{:S(2)}, u32[]{:S(2)}) collective-permute-start(f32[34,34,1]{1,0,2:T(8,128)S(1)} %copy.361), channel_id=1, source_target_pairs={{1,0},{3,2},{5,4},{7,6},{9,8},{11,10},{13,12},{15,14},{17,16},{19,... | collective-permute-start | bytes 13880 | tf_op jit(solution)/shard_map/ppermute | solution.py:20
  265.1 13.6 %copy-start = (f32[32,32,128]{2,1,0:T(8,128)}, f32[32,32,128]{2,1,0:T(8,128)S(1)}, u32[]{:S(2)}) copy-start(f32[32,32,128]{2,1,0:T(8,128)S(1)} %fusion.23) | copy-start | bytes 1572868
  265.1 5.3 %collective-permute-start.30 = (f32[1,32,128]{2,1,0:T(8,128)S(1)}, f32[1,32,128]{2,1,0:T(8,128)S(1)}, u32[]{:S(2)}, u32[]{:S(2)}) collective-permute-start(f32[1,32,128]{2,1,0:T(8,128)S(1)} %get-tuple-element.47), channel_id=1, source_target_pairs={{8,0},{16,8},{24,16},{9,1},{17,9},{25,17},{10,2},{18,10},{26,18},{... | collective-permute-start | bytes 49160 | tf_op jit(solution)/shard_map/ppermute | solution.py:20
  267.1 5.4 %collective-permute-start.31 = (f32[1,32,128]{2,1,0:T(8,128)S(1)}, f32[1,32,128]{2,1,0:T(8,128)S(1)}, u32[]{:S(2)}, u32[]{:S(2)}) collective-permute-start(f32[1,32,128]{2,1,0:T(8,128)S(1)} %get-tuple-element.46), channel_id=1, source_target_pairs={{0,8},{8,16},{16,24},{1,9},{9,17},{17,25},{2,10},{10,18},{18,26},{... | collective-permute-start | bytes 49160 | tf_op jit(solution)/shard_map/ppermute | solution.py:17
  272.5 3.0 %collective-permute-start.32 = (f32[34,1,128]{2,0,1:T(8,128)S(1)}, f32[34,1,128]{2,0,1:T(8,128)S(1)}, u32[]{:S(2)}, u32[]{:S(2)}) collective-permute-start(f32[34,1,128]{2,0,1:T(8,128)S(1)} %copy.365), channel_id=1, source_target_pairs={{2,0},{4,2},{6,4},{3,1},{5,3},{7,5},{10,8},{12,10},{14,12},{11,9},... | collective-permute-start | bytes 52232 | tf_op jit(solution)/shard_map/ppermute | solution.py:20
  274.2 4.5 %collective-permute-start.33 = (f32[34,1,128]{2,0,1:T(8,128)S(1)}, f32[34,1,128]{2,0,1:T(8,128)S(1)}, u32[]{:S(2)}, u32[]{:S(2)}) collective-permute-start(f32[34,1,128]{2,0,1:T(8,128)S(1)} %copy.367), channel_id=1, source_target_pairs={{0,2},{2,4},{4,6},{1,3},{3,5},{5,7},{8,10},{10,12},{12,14},{9,11},... | collective-permute-start | bytes 52232 | tf_op jit(solution)/shard_map/ppermute | solution.py:17
  281.6 7.2 %collective-permute-start.35 = (f32[34,34,1]{1,0,2:T(8,128)S(1)}, f32[34,34,1]{1,0,2:T(8,128)S(1)}, u32[]{:S(2)}, u32[]{:S(2)}) collective-permute-start(f32[34,34,1]{1,0,2:T(8,128)S(1)} %copy.373), channel_id=1, source_target_pairs={{0,1},{2,3},{4,5},{6,7},{8,9},{10,11},{12,13},{14,15},{16,17},{18,... | collective-permute-start | bytes 13880 | tf_op jit(solution)/shard_map/ppermute | solution.py:17
  284.4 5.7 %collective-permute-start.34 = (f32[34,34,1]{1,0,2:T(8,128)S(1)}, f32[34,34,1]{1,0,2:T(8,128)S(1)}, u32[]{:S(2)}, u32[]{:S(2)}) collective-permute-start(f32[34,34,1]{1,0,2:T(8,128)S(1)} %copy.371), channel_id=1, source_target_pairs={{1,0},{3,2},{5,4},{7,6},{9,8},{11,10},{13,12},{15,14},{17,16},{19,... | collective-permute-start | bytes 13880 | tf_op jit(solution)/shard_map/ppermute | solution.py:20
where the time goes:
time: 298 us; the launch traced here: 296 us
  starting transfers between devices  102 us (34%)
  local copies, waits for them, and re-layouts  86.6 us (29%)
  waiting for transfers between devices  39.7 us (13%)
  blocking collectives  33.1 us (11%)
  other arithmetic  32.4 us (11%)
    ppermute x18, starting transfers between devices, extended(): lax.ppermute(lax.slice_in_dim(block, 0, width, axis=dim), axis, backward)  57.1 us
    ppermute x18, starting transfers between devices, extended(): lax.ppermute(lax.slice_in_dim(block, block.shape[dim] - width, None, axis...  34.4 us
    ppermute x18, waiting for transfers between devices, extended(): lax.ppermute(lax.slice_in_dim(block, block.shape[dim] - width, None, axis...  23.4 us
    reshape x7, local copies, waits for them, and re-layouts, to_block(): grouped = picked.reshape(BXB, BYB, BZB, box_edge, box_edge, box_edge)  21.9 us
    slice x22, local copies, waits for them, and re-layouts, extended(): lax.slice_in_dim(block, 0, width, axis=dim)  17.8 us
    all_to_all x1, blocking collectives, per_device(): lax.all_to_all(sol_sent, 'gy', split_axis=0, concat_axis=0, tiled=True)  16.6 us
    all_to_all x1, blocking collectives, per_device(): lax.all_to_all(diffuse_sent, 'gy', split_axis=0, concat_axis=0, tiled=True)  16.5 us
    select_n x4, other arithmetic, per_device(): solution = jnp.where(parity == colour, updated, solution)  15.8 us
  transfers between devices with their start and end apart: 38, of which 11 were waited for; matrix products, arithmetic and copies ran while one was open for 20% of the time, Pallas kernels for 0%

commit v1 on v0

v1 whole, which is shorter than its diff:
```python
import functools

import jax
import jax.numpy as jnp
from jax import lax
from jax.experimental import pallas as pl
from jax.experimental.pallas import tpu as pltpu
from jax.sharding import PartitionSpec as P

SWEEPS = 2
E = 32
L = 128
PER = 4
MESH = pl.DeviceIdType.MESH
SIDES = (("gx", -1), ("gx", 1), ("gy", -1), ("gy", 1), ("gz", -1), ("gz", 1))


def kernel(
    width,
    corners,
    sol_in,
    rhs_in,
    abs_in,
    dif_in,
    sol_out,
    res_out,
    own_b,
    own_u,
    own_a,
    own_f,
    st_b,
    st_u,
    st_a,
    st_f,
    rv_b,
    rv_u,
    rv_a,
    rv_f,
    b,
    u,
    f,
    dia,
    inv,
    res,
    cxl,
    cxh,
    cy,
    czl,
    czh,
    hs,
    hr,
    in_sem,
    ms_sem,
    mr_sem,
    hs_sem,
    hr_sem,
):
    me = {axis: lax.axis_index(axis) for axis in ("gx", "gy", "gz")}
    n_y = width["gy"]
    my_y = me["gy"]

    loads = [
        pltpu.make_async_copy(src, dst, in_sem.at[i])
        for i, (src, dst) in enumerate(
            ((dif_in, own_b), (sol_in, own_u), (abs_in, own_a), (rhs_in, own_f))
        )
    ]
    for load in loads:
        load.start()

    def exists(side):
        axis, step = SIDES[side]
        return me[axis] > 0 if step < 0 else me[axis] < width[axis] - 1

    hr[...] = jnp.zeros_like(hr)

    barrier = pltpu.get_barrier_semaphore()
    partners = n_y - 1
    for k in range(1, n_y):
        pl.semaphore_signal(
            barrier, inc=1, device_id={"gy": lax.rem(my_y + k, n_y)}, device_id_type=MESH
        )
    for side in (0, 1, 4, 5):
        axis, step = SIDES[side]

        @pl.when(exists(side))
        def _():
            pl.semaphore_signal(
                barrier, inc=1, device_id={axis: me[axis] + step}, device_id_type=MESH
            )

        partners = partners + exists(side).astype(jnp.int32)

    def owner_inner(device, slot):
        row = ((me["gx"] * n_y + device) * width["gz"] + me["gz"]) * PER + slot
        return corners[1, row] // E, lax.rem(corners[2, row], PER * E) // E

    mine = [owner_inner(my_y, s) for s in range(PER)]
    send_slot = []
    for k in range(1, n_y):
        target = lax.rem(my_y + k, n_y)
        slot = jnp.int32(0)
        for s in range(PER):
            slot = jnp.where(mine[s][0] == target, s, slot)
        send_slot.append(slot)
    own_slot = [jnp.int32(0)] * PER
    is_own = [jnp.int32(0)] * PER
    got_slot = [jnp.int32(0)] * PER
    for q in range(PER):
        for s in range(PER):
            here = (mine[s][0] == my_y) & (mine[s][1] == q)
            own_slot[q] = jnp.where(here, s, own_slot[q])
            is_own[q] = jnp.where(here, 1, is_own[q])
    for k in range(1, n_y):
        device = lax.rem(my_y + n_y - k, n_y)
        for s in range(PER):
            owner, inner = owner_inner(device, s)
            for q in range(PER):
                got_slot[q] = jnp.where((owner == my_y) & (inner == q), k - 1, got_slot[q])

    row = lax.broadcasted_iota(jnp.int32, (E, L), 0)
    lane = lax.broadcasted_iota(jnp.int32, (E, L), 1)
    wide_row = lax.broadcasted_iota(jnp.int32, (E // 2, E * E), 0)
    wide_lane = lax.broadcasted_iota(jnp.int32, (E // 2, E * E), 1)
    odd_half = (wide_row + wide_lane // E + wide_lane) % 2 == 1

    def migrate(i, k, st, rv):
        return pltpu.make_async_remote_copy(
            src_ref=st.at[k - 1],
            dst_ref=rv.at[k - 1],
            send_sem=ms_sem.at[i, k - 1],
            recv_sem=mr_sem.at[i, k - 1],
            device_id={"gy": lax.rem(my_y + k, n_y)},
            device_id_type=MESH,
        )

    fields = ((own_b, st_b, rv_b), (own_u, st_u, rv_u), (own_a, st_a, rv_a), (own_f, st_f, rv_f))
    for i, (own, st, rv) in enumerate(fields):
        loads[i].wait()
        for k in range(1, n_y):
            box = own[send_slot[k - 1]]
            if i == 1:
                box = jnp.where(odd_half, box[: E // 2], pltpu.roll(box[E // 2 :], 1, 0))
            st[k - 1] = box
        if i == 0:
            pl.semaphore_wait(barrier, partners)
        for k in range(1, n_y):
            migrate(i, k, st, rv).start()

    def arrived(i):
        _, st, rv = fields[i]
        for k in range(1, n_y):
            migrate(i, k, st, rv).wait_recv()

    group = lane // E
    own_mask = [jnp.full((E, L), is_own[q], jnp.int32) == 1 for q in range(PER)]

    def assembled(i, put):
        own, _, rv = fields[i]

        def columns(t, carry):
            at = pl.ds(pl.multiple_of(t * L, L), L)
            parts = []
            for q in range(PER):
                got = rv[got_slot[q], :, at]
                if i == 1:
                    got = jnp.concatenate([got, pltpu.roll(got, E // 2 - 1, 0)], axis=0)
                parts.append(jnp.where(own_mask[q], own[own_slot[q], :, at], got))
            for j in range(PER):
                plane = parts[j]
                for q in range(PER):
                    if q != j:
                        plane = jnp.where(
                            group == q, pltpu.roll(parts[q], (q - j) * E % L, 1), plane
                        )
                put(t * PER + j, plane)
            return carry

        lax.fori_loop(0, E * E // L, columns, 0)

    def at_plane(y):
        return pl.ds(pl.multiple_of(y * E, E), E)

    def z_face(y, v, low, high):
        low = jnp.where(lane == y, pltpu.roll(v, y, 1), low)
        high = jnp.where(lane == y, pltpu.roll(v, y + 1, 1), high)
        return low, high

    def pack_z(ref):
        def planes(t, faces):
            for j in range(4):
                y = t * 4 + j
                faces = z_face(y, ref[at_plane(y + 1), :], *faces)
            return faces

        zero = jnp.zeros((E, L), jnp.float32)
        return lax.fori_loop(0, E // 4, planes, (zero, zero))

    def face_copy(e, side):
        axis, step = SIDES[side]
        return pltpu.make_async_remote_copy(
            src_ref=hs.at[e, side],
            dst_ref=hr.at[e, side ^ 1],
            send_sem=hs_sem.at[e, side],
            recv_sem=hr_sem.at[e, side ^ 1],
            device_id={axis: me[axis] + step},
            device_id_type=MESH,
        )

    def send_faces(e, ref, z_faces):
        hs[e, 0] = ref[pl.ds(E, E, stride=E), :]
        hs[e, 1] = ref[pl.ds(2 * E - 1, E, stride=E), :]
        hs[e, 2] = ref[pl.ds(E, E), :]
        hs[e, 3] = ref[pl.ds(E * E, E), :]
        hs[e, 4] = z_faces[0]
        hs[e, 5] = z_faces[1]
        for side in range(6):

            @pl.when(exists(side))
            def _():
                face_copy(e, side).start()

    def take_faces(e, ref):
        for side in range(6):
            axis, step = SIDES[side]

            @pl.when(exists(side))
            def _():
                pltpu.make_async_remote_copy(
                    src_ref=hs.at[e, side],
                    dst_ref=hr.at[e, side],
                    send_sem=hs_sem.at[e, side],
                    recv_sem=hr_sem.at[e, side],
                    device_id={axis: me[axis] + step},
                    device_id_type=MESH,
                ).wait_recv()

        ref[pl.ds(0, E), :] = hr[e, 2]
        ref[pl.ds((E + 1) * E, E), :] = hr[e, 3]

    def around(e, ref, y):
        v = ref[at_plane(y + 1), :]
        x_low = jnp.where(row == 0, hr[e, 0, pl.ds(y, 1), :], pltpu.roll(v, 1, 0))
        x_high = jnp.where(row == E - 1, hr[e, 1, pl.ds(y, 1), :], pltpu.roll(v, E - 1, 0))
        y_low = ref[at_plane(y), :]
        y_high = ref[at_plane(y + 2), :]
        z_low = jnp.where(
            lane == 0, pltpu.roll(hr[e, 4], lax.rem(L - y, L), 1), pltpu.roll(v, 1, 1)
        )
        z_high = jnp.where(
            lane == L - 1, pltpu.roll(hr[e, 5], L - 1 - y, 1), pltpu.roll(v, L - 1, 1)
        )
        return v, x_low, x_high, y_low, y_high, z_low, z_high

    arrived(0)

    def put_b(y, plane):
        b[at_plane(y + 1), :] = plane

    assembled(0, put_b)
    send_faces(0, b, pack_z(b))

    arrived(1)

    def put_u(y, plane):
        u[at_plane(y + 1), :] = plane

    assembled(1, put_u)
    send_faces(1, u, pack_z(u))

    take_faces(0, b)

    def coefs(y, carry):
        v, x_low, x_high, y_low, y_high, z_low, z_high = around(0, b, y)
        at = at_plane(y)
        x_low = 0.5 * (x_low + v)
        x_high = 0.5 * (x_high + v)
        y_low = 0.5 * (y_low + v)
        y_high = 0.5 * (y_high + v)
        z_low = 0.5 * (z_low + v)
        z_high = 0.5 * (z_high + v)
        cxl[at, :] = x_low
        cxh[at, :] = x_high
        cy[at, :] = y_low
        cy[at_plane(y + 1), :] = y_high
        czl[at, :] = z_low
        czh[at, :] = z_high
        dia[at, :] = (x_high + x_low) + (y_high + y_low) + (z_high + z_low)
        return carry

    lax.fori_loop(0, E, coefs, 0)

    arrived(2)

    def put_a(y, plane):
        at = at_plane(y)
        total = plane + dia[at, :]
        dia[at, :] = total
        inv[at, :] = 1.0 / total

    assembled(2, put_a)
    arrived(3)

    def put_f(y, plane):
        f[at_plane(y), :] = plane

    assembled(3, put_f)

    def neighbours(e, y):
        v, x_low, x_high, y_low, y_high, z_low, z_high = around(e, u, y)
        at = at_plane(y)
        total = cxh[at, :] * x_high + cxl[at, :] * x_low
        total = total + (cy[at_plane(y + 1), :] * y_high + cy[at, :] * y_low)
        total = total + (czh[at, :] * z_high + czl[at, :] * z_low)
        return v, total

    e = 1
    for sweep in range(SWEEPS):
        for colour in (0, 1):
            take_faces(e, u)

            def planes(t, faces):
                for j in range(4):
                    y = t * 4 + j
                    at = at_plane(y)
                    v, total = neighbours(e, y)
                    new = (f[at, :] + total) * inv[at, :]
                    v = jnp.where((row + lane + j) % 2 == colour, new, v)
                    u[at_plane(y + 1), :] = v
                    faces = z_face(y, v, *faces)
                return faces

            zero = jnp.zeros((E, L), jnp.float32)
            faces = lax.fori_loop(0, E // 4, planes, (zero, zero))
            e += 1
            send_faces(e, u, faces)

    for x in range(E):
        sol_out[x] = u[pl.ds(E + x, E, stride=E), :]
    take_faces(e, u)

    def residual(y, carry):
        at = at_plane(y)
        v, total = neighbours(e, y)
        res[at, :] = f[at, :] - (dia[at, :] * v - total)
        return carry

    lax.fori_loop(0, E, residual, 0)
    for x in range(E):
        res_out[x] = res[pl.ds(x, E, stride=E), :]

    for i, (_, st, rv) in enumerate(fields):
        for k in range(1, n_y):
            migrate(i, k, st, rv).wait_send()
    for exchange in range(e + 1):
        for side in range(6):

            @pl.when(exists(side))
            def _():
                face_copy(exchange, side).wait_send()


def per_device(width, solution_old, right_side, acoef, bcoef, corners):
    n_y = width["gy"]
    exchanges = 2 + 2 * SWEEPS
    box = (E, E * E)
    field = pltpu.VMEM((E * E, L), jnp.float32)
    padded = pltpu.VMEM(((E + 2) * E, L), jnp.float32)
    faces = pltpu.VMEM((exchanges, 6, E, L), jnp.float32)
    own = pltpu.VMEM((PER,) + box, jnp.float32)
    moved = pltpu.VMEM((n_y - 1,) + box, jnp.float32)
    half = pltpu.VMEM((n_y - 1, E // 2, E * E), jnp.float32)
    out = jax.ShapeDtypeStruct((E, E, L), jnp.float32)
    return pl.pallas_call(
        functools.partial(kernel, width),
        out_shape=(out, out),
        in_specs=[pl.BlockSpec(memory_space=pltpu.SMEM)]
        + [pl.BlockSpec(memory_space=pl.ANY)] * 4,
        out_specs=(pl.BlockSpec(memory_space=pltpu.VMEM),) * 2,
        scratch_shapes=[own] * 4
        + [moved, half, moved, moved] * 2
        + [padded, padded]
        + [field] * 6
        + [pltpu.VMEM(((E + 1) * E, L), jnp.float32)]
        + [field] * 2
        + [faces] * 2
        + [
            pltpu.SemaphoreType.DMA((4,)),
            pltpu.SemaphoreType.DMA((4, n_y - 1)),
            pltpu.SemaphoreType.DMA((4, n_y - 1)),
            pltpu.SemaphoreType.DMA((exchanges, 6)),
            pltpu.SemaphoreType.DMA((exchanges, 6)),
        ],
        compiler_params=pltpu.CompilerParams(
            collective_id=0, has_side_effects=True, vmem_limit_bytes=40 * 1024 * 1024
        ),
        cost_estimate=pl.CostEstimate(
            flops=100 * E * E * L, bytes_accessed=24 * E * E * L, transcendentals=0
        ),
    )(corners, solution_old, right_side, acoef, bcoef)


def solution(mesh):
    width = dict(mesh.shape)
    boxes = P(("gx", "gy", "gz"), None, None)
    level = P("gx", "gy", "gz")
    return jax.shard_map(
        functools.partial(per_device, width),
        mesh=mesh,
        in_specs=(boxes, boxes, boxes, boxes, P()),
        out_specs=(level, level),
        check_vma=False,
    )
```

time: 298 us -> 82.1 us (0.28)
  the two profiles are of different devices: /device:TPU:29 before, /device:TPU:0 now
where the time goes in v1:
time: 82.1 us; the launch traced here: 81.8 us
  Pallas kernels  74.7 us (91%)
  local copies, waits for them, and re-layouts  6.43 us (8%)
    pallas_call x1, Pallas kernels, per_device(): pl.pallas_call(functools.partial(kernel, width), out_shape=(out, out), in...  74.7 us
    unnamed x12, local copies, waits for them, and re-layouts  6.43 us

profile of v1, /device:TPU:0, one launch (start us, length us, event | category | flops | bytes accessed | tf_op | source)
XLA Modules:
  0.0 81.8 jit_solution(1039699345763795650)
XLA Ops:
  0.6 0.0 copy-start
  0.6 1.0 %copy-done = f32[4,32,1024]{2,1,0:T(8,128)S(1)} copy-done((f32[4,32,1024]{2,1,0:T(8,128)S(1)}, f32[4,32,1024]{2,1,0:T(8,128)}, u32[]{:S(2)}) %copy-start) | copy-done | bytes 524312
  1.7 0.0 copy-start.1
  1.7 1.0 %copy-done.1 = f32[4,32,1024]{2,1,0:T(8,128)S(1)} copy-done((f32[4,32,1024]{2,1,0:T(8,128)S(1)}, f32[4,32,1024]{2,1,0:T(8,128)}, u32[]{:S(2)}) %copy-start.1) | copy-done | bytes 524312
  2.7 0.0 copy-start.2
  2.7 1.0 %copy-done.2 = f32[4,32,1024]{2,1,0:T(8,128)S(1)} copy-done((f32[4,32,1024]{2,1,0:T(8,128)S(1)}, f32[4,32,1024]{2,1,0:T(8,128)}, u32[]{:S(2)}) %copy-start.2) | copy-done | bytes 524312
  3.8 0.0 copy-start.3
  3.8 1.0 %copy-done.3 = f32[4,32,1024]{2,1,0:T(8,128)S(1)} copy-done((f32[4,32,1024]{2,1,0:T(8,128)S(1)}, f32[4,32,1024]{2,1,0:T(8,128)}, u32[]{:S(2)}) %copy-start.3) | copy-done | bytes 524312
  4.8 0.0 copy-start.4
  4.8 0.7 copy-done.4
  5.5 74.7 %shard_map.68 = (f32[32,32,128]{2,1,0:T(8,128)S(1)}, f32[32,32,128]{2,1,0:T(8,128)S(1)}) custom-call(s32[3,128]{1,0:T(4,128)S(1)} %copy-done.4, f32[4,32,1024]{2,1,0:T(8,128)S(1)} %copy-done, f32[4,32,1024]{2,1,0:T(8,128)S(1)} %copy-done.1, f32[4,32,1024]{2,1,0:T(8,128)S(1)} %copy-done.2, f32[4,32,1024]{2,1,0:T(8,128)S(1)} %copy-done.3), custom_call_target="tpu_custom_call" | custom-call | flops 13107200 | bytes 3145728 | tf_op jit(solution)/shard_map/pallas_call | solution.py:374
  80.2 0.8 copy.9
  81.0 0.8 copy.10
Async XLA Ops:
  0.6 1.0 %copy-start = (f32[4,32,1024]{2,1,0:T(8,128)S(1)}, f32[4,32,1024]{2,1,0:T(8,128)}, u32[]{:S(2)}) copy-start(f32[4,32,1024]{2,1,0:T(8,128)} %sol_in.1) | copy-start | bytes 1572868
  1.7 1.0 %copy-start.1 = (f32[4,32,1024]{2,1,0:T(8,128)S(1)}, f32[4,32,1024]{2,1,0:T(8,128)}, u32[]{:S(2)}) copy-start(f32[4,32,1024]{2,1,0:T(8,128)} %rhs_in.1) | copy-start | bytes 1572868
  2.7 1.0 %copy-start.2 = (f32[4,32,1024]{2,1,0:T(8,128)S(1)}, f32[4,32,1024]{2,1,0:T(8,128)}, u32[]{:S(2)}) copy-start(f32[4,32,1024]{2,1,0:T(8,128)} %abs_in.1) | copy-start | bytes 1572868
  3.8 1.0 %copy-start.3 = (f32[4,32,1024]{2,1,0:T(8,128)S(1)}, f32[4,32,1024]{2,1,0:T(8,128)}, u32[]{:S(2)}) copy-start(f32[4,32,1024]{2,1,0:T(8,128)} %dif_in.1) | copy-start | bytes 1572868
  4.8 0.7 copy-start.4

commit v2 on v1

--- a/solution.py
+++ b/solution.py
@@ -11,6 +11,7 @@
 E = 32
 L = 128
 PER = 4
+ST = E + 8
 MESH = pl.DeviceIdType.MESH
 SIDES = (("gx", -1), ("gx", 1), ("gy", -1), ("gy", 1), ("gz", -1), ("gz", 1))
 
@@ -47,6 +48,8 @@
     cy,
     czl,
     czh,
+    ez,
+    ezi,
     hs,
     hr,
     in_sem,
@@ -73,6 +76,8 @@
         return me[axis] > 0 if step < 0 else me[axis] < width[axis] - 1
 
     hr[...] = jnp.zeros_like(hr)
+    b[...] = jnp.zeros_like(b)
+    u[...] = jnp.zeros_like(u)
 
     barrier = pltpu.get_barrier_semaphore()
     partners = n_y - 1
@@ -93,7 +98,7 @@
 
     def owner_inner(device, slot):
         row = ((me["gx"] * n_y + device) * width["gz"] + me["gz"]) * PER + slot
-        return corners[1, row] // E, lax.rem(corners[2, row], PER * E) // E
+        return lax.div(corners[1, row], E), lax.div(lax.rem(corners[2, row], PER * E), E)
 
     mine = [owner_inner(my_y, s) for s in range(PER)]
     send_slot = []
@@ -181,20 +186,35 @@
     def at_plane(y):
         return pl.ds(pl.multiple_of(y * E, E), E)
 
-    def z_face(y, v, low, high):
-        low = jnp.where(lane == y, pltpu.roll(v, y, 1), low)
-        high = jnp.where(lane == y, pltpu.roll(v, y + 1, 1), high)
-        return low, high
-
-    def pack_z(ref):
-        def planes(t, faces):
+    def base(y):
+        return pl.multiple_of(y * ST + ST + 8, 8)
+
+    def padded(y):
+        return pl.ds(base(y), E)
+
+    even = (row + lane) % 2 == 0
+    odd = (row + lane) % 2 == 1
+    pair = lane // 2
+    zero = jnp.zeros((E, L), jnp.float32)
+    first = ST + 8
+
+    def pack_z(y, v, face):
+        return jnp.where(pair == y, pltpu.roll(v, 2 * y + 1, 1), face)
+
+    def pack_all_z(ref):
+        def planes(t, face):
             for j in range(4):
                 y = t * 4 + j
-                faces = z_face(y, ref[at_plane(y + 1), :], *faces)
-            return faces
-
-        zero = jnp.zeros((E, L), jnp.float32)
-        return lax.fori_loop(0, E // 4, planes, (zero, zero))
+                face = pack_z(y, ref[padded(y), :], face)
+            return face
+
+        return lax.fori_loop(0, E // 4, planes, zero)
+
+    def z_halo(e):
+        return jnp.where(lane % 2 == 0, hr[e, 4], pltpu.roll(hr[e, 5], L - 2, 1))
+
+    def z_edge(halo, y):
+        return pltpu.roll(halo, lax.rem(L - 2 * y, L), 1)
 
     def face_copy(e, side):
         axis, step = SIDES[side]
@@ -207,20 +227,20 @@
             device_id_type=MESH,
         )
 
-    def send_faces(e, ref, z_faces):
-        hs[e, 0] = ref[pl.ds(E, E, stride=E), :]
-        hs[e, 1] = ref[pl.ds(2 * E - 1, E, stride=E), :]
-        hs[e, 2] = ref[pl.ds(E, E), :]
-        hs[e, 3] = ref[pl.ds(E * E, E), :]
-        hs[e, 4] = z_faces[0]
-        hs[e, 5] = z_faces[1]
+    def send_faces(e, ref, z_face):
+        hs[e, 0] = ref[pl.ds(first, E, stride=ST), :]
+        hs[e, 1] = ref[pl.ds(first + E - 1, E, stride=ST), :]
+        hs[e, 2] = ref[pl.ds(first, E), :]
+        hs[e, 3] = ref[pl.ds(first + (E - 1) * ST, E), :]
+        hs[e, 4] = z_face
+        hs[e, 5] = z_face
         for side in range(6):
 
             @pl.when(exists(side))
             def _():
                 face_copy(e, side).start()
 
-    def take_faces(e, ref):
+    def wait_faces(e):
         for side in range(6):
             axis, step = SIDES[side]
 
@@ -235,56 +255,46 @@
                     device_id_type=MESH,
                 ).wait_recv()
 
-        ref[pl.ds(0, E), :] = hr[e, 2]
-        ref[pl.ds((E + 1) * E, E), :] = hr[e, 3]
-
-    def around(e, ref, y):
-        v = ref[at_plane(y + 1), :]
-        x_low = jnp.where(row == 0, hr[e, 0, pl.ds(y, 1), :], pltpu.roll(v, 1, 0))
-        x_high = jnp.where(row == E - 1, hr[e, 1, pl.ds(y, 1), :], pltpu.roll(v, E - 1, 0))
-        y_low = ref[at_plane(y), :]
-        y_high = ref[at_plane(y + 2), :]
-        z_low = jnp.where(
-            lane == 0, pltpu.roll(hr[e, 4], lax.rem(L - y, L), 1), pltpu.roll(v, 1, 1)
-        )
-        z_high = jnp.where(
-            lane == L - 1, pltpu.roll(hr[e, 5], L - 1 - y, 1), pltpu.roll(v, L - 1, 1)
-        )
-        return v, x_low, x_high, y_low, y_high, z_low, z_high
-
     arrived(0)
 
     def put_b(y, plane):
-        b[at_plane(y + 1), :] = plane
+        b[padded(y), :] = plane
 
     assembled(0, put_b)
-    send_faces(0, b, pack_z(b))
+    send_faces(0, b, pack_all_z(b))
 
     arrived(1)
 
     def put_u(y, plane):
-        u[at_plane(y + 1), :] = plane
+        u[padded(y), :] = plane
 
     assembled(1, put_u)
-    send_faces(1, u, pack_z(u))
-
-    take_faces(0, b)
+    send_faces(1, u, pack_all_z(u))
+
+    wait_faces(0)
+    b[pl.ds(first - 1, E, stride=ST), :] = hr[0, 0]
+    b[pl.ds(first + E, E, stride=ST), :] = hr[0, 1]
+    b[pl.ds(8, E), :] = hr[0, 2]
+    b[pl.ds(first + E * ST, E), :] = hr[0, 3]
+    b_halo = z_halo(0)
 
     def coefs(y, carry):
-        v, x_low, x_high, y_low, y_high, z_low, z_high = around(0, b, y)
+        v = b[padded(y), :]
         at = at_plane(y)
-        x_low = 0.5 * (x_low + v)
-        x_high = 0.5 * (x_high + v)
-        y_low = 0.5 * (y_low + v)
-        y_high = 0.5 * (y_high + v)
-        z_low = 0.5 * (z_low + v)
-        z_high = 0.5 * (z_high + v)
+        edge = z_edge(b_halo, y)
+        x_low = 0.5 * (b[pl.ds(base(y) - 1, E), :] + v)
+        x_high = 0.5 * (b[pl.ds(base(y) + 1, E), :] + v)
+        y_low = 0.5 * (b[padded(y - 1), :] + v)
+        y_high = 0.5 * (b[padded(y + 1), :] + v)
+        z_low = 0.5 * (jnp.where(lane == 0, edge, pltpu.roll(v, 1, 1)) + v)
+        z_high = 0.5 * (jnp.where(lane == L - 1, edge, pltpu.roll(v, L - 1, 1)) + v)
         cxl[at, :] = x_low
         cxh[at, :] = x_high
         cy[at, :] = y_low
         cy[at_plane(y + 1), :] = y_high
-        czl[at, :] = z_low
-        czh[at, :] = z_high
+        czl[at, :] = jnp.where(lane == 0, 0.0, z_low)
+        czh[at, :] = jnp.where(lane == L - 1, 0.0, z_high)
+        ez[at, :] = jnp.where(lane == 0, z_low, jnp.where(lane == L - 1, z_high, 0.0))
         dia[at, :] = (x_high + x_low) + (y_high + y_low) + (z_high + z_low)
         return carry
 
@@ -295,8 +305,10 @@
     def put_a(y, plane):
         at = at_plane(y)
         total = plane + dia[at, :]
+        inverse = 1.0 / total
         dia[at, :] = total
-        inv[at, :] = 1.0 / total
+        inv[at, :] = inverse
+        ezi[at, :] = ez[at, :] * inverse
 
     assembled(2, put_a)
     arrived(3)
@@ -306,46 +318,87 @@
 
     assembled(3, put_f)
 
-    def neighbours(e, y):
-        v, x_low, x_high, y_low, y_high, z_low, z_high = around(e, u, y)
+    def neighbours(y):
         at = at_plane(y)
-        total = cxh[at, :] * x_high + cxl[at, :] * x_low
-        total = total + (cy[at_plane(y + 1), :] * y_high + cy[at, :] * y_low)
-        total = total + (czh[at, :] * z_high + czl[at, :] * z_low)
-        return v, total
+        v = u[padded(y), :]
+        x_sum = cxh[at, :] * u[pl.ds(base(y) + 1, E), :] + cxl[at, :] * u[pl.ds(base(y) - 1, E), :]
+        y_sum = cy[at_plane(y + 1), :] * u[padded(y + 1), :] + cy[at, :] * u[padded(y - 1), :]
+        z_sum = czh[at, :] * pltpu.roll(v, L - 1, 1) + czl[at, :] * pltpu.roll(v, 1, 1)
+        return v, x_sum + y_sum + z_sum
+
+    low_x = pl.ds(0, E, stride=E)
+    high_x = pl.ds(E - 1, E, stride=E)
+    low_y = pl.ds(0, E)
+    high_y = pl.ds((E - 1) * E, E)
+    top_y = pl.ds(E * E, E)
 
     e = 1
     for sweep in range(SWEEPS):
         for colour in (0, 1):
-            take_faces(e, u)
-
-            def planes(t, faces):
+            masks = (even, odd) if colour == 0 else (odd, even)
+
+            def planes(t, carry):
                 for j in range(4):
                     y = t * 4 + j
                     at = at_plane(y)
-                    v, total = neighbours(e, y)
+                    v, total = neighbours(y)
                     new = (f[at, :] + total) * inv[at, :]
-                    v = jnp.where((row + lane + j) % 2 == colour, new, v)
-                    u[at_plane(y + 1), :] = v
-                    faces = z_face(y, v, *faces)
-                return faces
-
-            zero = jnp.zeros((E, L), jnp.float32)
-            faces = lax.fori_loop(0, E // 4, planes, (zero, zero))
+                    u[padded(y), :] = jnp.where(masks[j % 2], new, v)
+                return carry
+
+            lax.fori_loop(0, E // 4, planes, 0)
+            wait_faces(e)
+            for at, mask, term in (
+                (pl.ds(first, E, stride=ST), 0, cxl[low_x, :] * inv[low_x, :] * hr[e, 0]),
+                (pl.ds(first + E - 1, E, stride=ST), 1, cxh[high_x, :] * inv[high_x, :] * hr[e, 1]),
+                (pl.ds(first, E), 0, cy[low_y, :] * inv[low_y, :] * hr[e, 2]),
+                (pl.ds(first + (E - 1) * ST, E), 1, cy[top_y, :] * inv[high_y, :] * hr[e, 3]),
+            ):
+                u[at, :] = u[at, :] + jnp.where(masks[mask], term, 0.0)
+            halo = z_halo(e)
+
+            def edges(t, face):
+                for j in range(4):
+                    y = t * 4 + j
+                    term = ezi[at_plane(y), :] * z_edge(halo, y)
+                    v = u[padded(y), :] + jnp.where(masks[j % 2], term, 0.0)
+                    u[padded(y), :] = v
+                    face = pack_z(y, v, face)
+                return face
+
+            face = lax.fori_loop(0, E // 4, edges, zero)
             e += 1
-            send_faces(e, u, faces)
-
+            send_faces(e, u, face)
+
+    def residual(t, carry):
+        for j in range(4):
+            y = t * 4 + j
+            at = at_plane(y)
+            v, total = neighbours(y)
+            res[at, :] = f[at, :] - (dia[at, :] * v - total)
+        return carry
+
+    lax.fori_loop(0, E // 4, residual, 0)
     for x in range(E):
-        sol_out[x] = u[pl.ds(E + x, E, stride=E), :]
-    take_faces(e, u)
-
-    def residual(y, carry):
-        at = at_plane(y)
-        v, total = neighbours(e, y)
-        res[at, :] = f[at, :] - (dia[at, :] * v - total)
+        sol_out[x] = u[pl.ds(first + x, E, stride=ST), :]
+    wait_faces(e)
+    for at, term in (
+        (low_x, cxl[low_x, :] * hr[e, 0]),
+        (high_x, cxh[high_x, :] * hr[e, 1]),
+        (low_y, cy[low_y, :] * hr[e, 2]),
+        (high_y, cy[top_y, :] * hr[e, 3]),
+    ):
+        res[at, :] = res[at, :] + term
+    last_halo = z_halo(e)
+
+    def last_edges(t, carry):
+        for j in range(4):
+            y = t * 4 + j
+            at = at_plane(y)
+            res[at, :] = res[at, :] + ez[at, :] * z_edge(last_halo, y)
         return carry
 
-    lax.fori_loop(0, E, residual, 0)
+    lax.fori_loop(0, E // 4, last_edges, 0)
     for x in range(E):
         res_out[x] = res[pl.ds(x, E, stride=E), :]
 
@@ -365,7 +418,7 @@
     exchanges = 2 + 2 * SWEEPS
     box = (E, E * E)
     field = pltpu.VMEM((E * E, L), jnp.float32)
-    padded = pltpu.VMEM(((E + 2) * E, L), jnp.float32)
+    padded = pltpu.VMEM(((E + 2) * ST + 16, L), jnp.float32)
     faces = pltpu.VMEM((exchanges, 6, E, L), jnp.float32)
     own = pltpu.VMEM((PER,) + box, jnp.float32)
     moved = pltpu.VMEM((n_y - 1,) + box, jnp.float32)
@@ -382,7 +435,7 @@
         + [padded, padded]
         + [field] * 6
         + [pltpu.VMEM(((E + 1) * E, L), jnp.float32)]
-        + [field] * 2
+        + [field] * 4
         + [faces] * 2
         + [
             pltpu.SemaphoreType.DMA((4,)),
@@ -392,7 +445,7 @@
             pltpu.SemaphoreType.DMA((exchanges, 6)),
         ],
         compiler_params=pltpu.CompilerParams(
-            collective_id=0, has_side_effects=True, vmem_limit_bytes=40 * 1024 * 1024
+            collective_id=0, has_side_effects=True, vmem_limit_bytes=64 * 1024 * 1024
         ),
         cost_estimate=pl.CostEstimate(
             flops=100 * E * E * L, bytes_accessed=24 * E * E * L, transcendentals=0

time: 82.1 us -> 76.7 us (0.934)
  local copies, waits for them, and re-layouts: 6.43 us -> 2.72 us
  Pallas kernels: 74.7 us -> 73.1 us
    unnamed x12 -> x4, local copies, waits for them, and re-layouts: 6.43 us -> 2.72 us
    pallas_call x1, Pallas kernels: 74.7 us -> 73.1 us  [per_device(): pl.pallas_call(functools.partial(kernel, width), out_shape=(out, out), in...]
where the time goes in v2:
time: 76.7 us; the launch traced here: 76.5 us
  Pallas kernels  73.1 us (95%)
  local copies, waits for them, and re-layouts  2.72 us (4%)
    pallas_call x1, Pallas kernels, per_device(): pl.pallas_call(functools.partial(kernel, width), out_shape=(out, out), in...  73.1 us
    unnamed x4, local copies, waits for them, and re-layouts  2.72 us

profile of v2, /device:TPU:0, one launch (start us, length us, event | category | flops | bytes accessed | tf_op | source)
XLA Modules:
  0.0 76.5 jit_solution(5565526605552854447)
XLA Ops:
  0.6 73.1 %shard_map.68 = (f32[32,32,128]{2,1,0:T(8,128)}, f32[32,32,128]{2,1,0:T(8,128)}) custom-call(s32[3,128]{1,0:T(4,128)} %corners.1, f32[4,32,1024]{2,1,0:T(8,128)} %sol_in.1, f32[4,32,1024]{2,1,0:T(8,128)} %rhs_in.1, f32[4,32,1024]{2,1,0:T(8,128)} %abs_in.1, f32[4,32,1024]{2,1,0:T(8,128)} %dif_in.1), custom_call_target="tpu_custom_call" | custom-call | flops 13107200 | bytes 3145728 | tf_op jit(solution)/shard_map/pallas_call | solution.py:427
  73.8 0.0 copy-start
  73.8 1.9 %copy.9 = f32[32,32,128]{2,1,0:T(8,128)} copy(f32[32,32,128]{2,1,0:T(8,128)} %get-tuple-element.4) | data formatting | bytes 1048576
  75.7 0.0 copy-done
  75.7 0.8 %copy.10 = f32[32,32,128]{2,1,0:T(8,128)} copy(f32[32,32,128]{2,1,0:T(8,128)S(1)} %copy-done) | data formatting | bytes 1048576
Async XLA Ops:
  73.8 1.9 %copy-start = (f32[32,32,128]{2,1,0:T(8,128)S(1)}, f32[32,32,128]{2,1,0:T(8,128)}, u32[]{:S(2)}) copy-start(f32[32,32,128]{2,1,0:T(8,128)} %get-tuple-element.5) | copy-start | bytes 1572868

commit v3 on v2

--- a/solution.py
+++ b/solution.py
@@ -80,12 +80,8 @@
     u[...] = jnp.zeros_like(u)
 
     barrier = pltpu.get_barrier_semaphore()
-    partners = n_y - 1
-    for k in range(1, n_y):
-        pl.semaphore_signal(
-            barrier, inc=1, device_id={"gy": lax.rem(my_y + k, n_y)}, device_id_type=MESH
-        )
-    for side in (0, 1, 4, 5):
+    partners = 0
+    for side in range(6):
         axis, step = SIDES[side]
 
         @pl.when(exists(side))
@@ -100,28 +96,40 @@
         row = ((me["gx"] * n_y + device) * width["gz"] + me["gz"]) * PER + slot
         return lax.div(corners[1, row], E), lax.div(lax.rem(corners[2, row], PER * E), E)
 
-    mine = [owner_inner(my_y, s) for s in range(PER)]
-    send_slot = []
-    for k in range(1, n_y):
-        target = lax.rem(my_y + k, n_y)
-        slot = jnp.int32(0)
-        for s in range(PER):
-            slot = jnp.where(mine[s][0] == target, s, slot)
-        send_slot.append(slot)
-    own_slot = [jnp.int32(0)] * PER
-    is_own = [jnp.int32(0)] * PER
-    got_slot = [jnp.int32(0)] * PER
-    for q in range(PER):
-        for s in range(PER):
-            here = (mine[s][0] == my_y) & (mine[s][1] == q)
-            own_slot[q] = jnp.where(here, s, own_slot[q])
-            is_own[q] = jnp.where(here, 1, is_own[q])
-    for k in range(1, n_y):
-        device = lax.rem(my_y + n_y - k, n_y)
-        for s in range(PER):
-            owner, inner = owner_inner(device, s)
-            for q in range(PER):
-                got_slot[q] = jnp.where((owner == my_y) & (inner == q), k - 1, got_slot[q])
+    table = [[owner_inner(j, s) for s in range(PER)] for j in range(n_y)]
+    goes, its_slot, its_inner = {}, {}, {}
+    for j in range(n_y):
+        for t in range(n_y):
+            if t != j:
+                live, slot, inner = jnp.int32(0), jnp.int32(0), jnp.int32(0)
+                for s in range(PER):
+                    hit = table[j][s][0] == t
+                    live = jnp.where(hit, 1, live)
+                    slot = jnp.where(hit, s, slot)
+                    inner = jnp.where(hit, table[j][s][1], inner)
+                goes[j, t], its_slot[j, t], its_inner[j, t] = live, slot, inner
+
+    n_slot = n_y - 1
+    rank = {}
+    code = [[jnp.int32(0)] * n_slot for _ in range(2)]
+    for way in range(2):
+        for c in range(n_y):
+            at = (lambda i: i) if way == 0 else (lambda i: n_y - 1 - i)
+            here = [jnp.int32(0)] * n_slot
+            count = jnp.int32(0)
+            for t in range(n_y - 1, c, -1):
+                for j in range(c + 1):
+                    pair = (at(j), at(t))
+                    rank[way, c, j, t] = count
+                    held = its_slot[pair] if j == c else PER + rank[way, c - 1, j, t]
+                    for k in range(n_slot):
+                        here[k] = jnp.where((goes[pair] == 1) & (count == k), held, here[k])
+                    count = count + goes[pair]
+            for k in range(n_slot):
+                code[way][k] = jnp.where(my_y == at(c), here[k], code[way][k])
+
+    inward = jnp.where(my_y < n_y // 2, 0, 1)
+    outward = 1 - inward
 
     row = lax.broadcasted_iota(jnp.int32, (E, L), 0)
     lane = lax.broadcasted_iota(jnp.int32, (E, L), 1)
@@ -129,33 +137,104 @@
     wide_lane = lax.broadcasted_iota(jnp.int32, (E // 2, E * E), 1)
     odd_half = (wide_row + wide_lane // E + wide_lane) % 2 == 1
 
-    def migrate(i, k, st, rv):
+    fields = ((own_b, st_b, rv_b), (own_u, st_u, rv_u), (own_a, st_a, rv_a), (own_f, st_f, rv_f))
+    chunks = (4, 1, 2, 2)
+
+    def part_of(ref, i, way, part):
+        if part == chunks[i]:
+            return ref.at[way, n_slot - 1]
+        rows = ref.shape[2] // chunks[i]
+        return ref.at[way, pl.ds(0, n_slot - 1), pl.ds(part * rows, rows)]
+
+    def hop(i, way, part, neighbour):
+        _, st, rv = fields[i]
         return pltpu.make_async_remote_copy(
-            src_ref=st.at[k - 1],
-            dst_ref=rv.at[k - 1],
-            send_sem=ms_sem.at[i, k - 1],
-            recv_sem=mr_sem.at[i, k - 1],
-            device_id={"gy": lax.rem(my_y + k, n_y)},
+            src_ref=part_of(st, i, way, part),
+            dst_ref=part_of(rv, i, way, part),
+            send_sem=ms_sem.at[i, way, part],
+            recv_sem=mr_sem.at[i, way, part],
+            device_id={"gy": neighbour},
             device_id_type=MESH,
         )
 
-    fields = ((own_b, st_b, rv_b), (own_u, st_u, rv_u), (own_a, st_a, rv_a), (own_f, st_f, rv_f))
-    for i, (own, st, rv) in enumerate(fields):
-        loads[i].wait()
-        for k in range(1, n_y):
-            box = own[send_slot[k - 1]]
-            if i == 1:
-                box = jnp.where(odd_half, box[: E // 2], pltpu.roll(box[E // 2 :], 1, 0))
-            st[k - 1] = box
-        if i == 0:
-            pl.semaphore_wait(barrier, partners)
-        for k in range(1, n_y):
-            migrate(i, k, st, rv).start()
+    def sends(way):
+        return jnp.where(way == 0, my_y < n_y - 1, my_y > 0)
+
+    def receives(way):
+        return jnp.where(way == 0, my_y > 0, my_y < n_y - 1)
+
+    def fill(i, way, k, start, rows):
+        own, st, rv = fields[i]
+        held = jnp.where(way == 0, code[0][k], code[1][k])
+        slot = jnp.where(held < PER, held, 0)
+        if i == 1:
+            box = own[slot]
+            box = jnp.where(odd_half, box[: E // 2], pltpu.roll(box[E // 2 :], 1, 0))
+        else:
+            box = own[slot, pl.ds(start, rows), :]
+        for r in range(n_slot - 1):
+            relayed = jnp.full((rows, E * E), held, jnp.int32) == PER + r
+            box = jnp.where(relayed, rv[way, r, pl.ds(start, rows), :], box)
+        st[way, k, pl.ds(start, rows), :] = box
+
+    def take_hop(i, way, part):
+        @pl.when(receives(way))
+        def _():
+            hop(i, way, part, my_y - 1 + 2 * way).wait_recv()
+
+    def pass_on(i, way, part):
+        rows = fields[i][1].shape[2]
+        if part < chunks[i]:
+            take_hop(i, way, part)
+            rows = rows // chunks[i]
+            for k in range(n_slot - 1):
+                fill(i, way, k, part * rows, rows)
+        else:
+            fill(i, way, n_slot - 1, 0, rows)
+
+        @pl.when(sends(way))
+        def _():
+            hop(i, way, part, my_y + 1 - 2 * way).start()
+
+    steps = [(i, part) for i in range(4) for part in range(chunks[i] + 1)]
+    lag = 2
+
+    def migrate(first_step, last_step):
+        for n in range(first_step, last_step):
+            if n < len(steps):
+                i, part = steps[n]
+                if part == 0:
+                    loads[i].wait()
+                if n == 0:
+                    pl.semaphore_wait(barrier, partners)
+                pass_on(i, inward, part)
+            if 0 <= n - lag < len(steps):
+                pass_on(steps[n - lag][0], outward, steps[n - lag][1])
 
     def arrived(i):
-        _, st, rv = fields[i]
-        for k in range(1, n_y):
-            migrate(i, k, st, rv).wait_recv()
+        for way in range(2):
+            take_hop(i, way, chunks[i])
+
+    migrate(0, 9)
+
+    own_slot = [jnp.int32(0)] * PER
+    is_own = [jnp.int32(0)] * PER
+    got_slot = [jnp.int32(0)] * PER
+    got_way = [jnp.int32(0)] * PER
+    for q in range(PER):
+        for s in range(PER):
+            owner, inner = owner_inner(my_y, s)
+            here = (owner == my_y) & (inner == q)
+            own_slot[q] = jnp.where(here, s, own_slot[q])
+            is_own[q] = jnp.where(here, 1, is_own[q])
+        for way in range(2):
+            for t in range(1, n_y):
+                for j in range(t):
+                    pair = (j, t) if way == 0 else (n_y - 1 - j, n_y - 1 - t)
+                    here = (goes[pair] == 1) & (its_inner[pair] == q) & (my_y == pair[1])
+                    slot = jnp.minimum(rank[way, t - 1, j, t], n_slot - 1)
+                    got_slot[q] = jnp.where(here, slot, got_slot[q])
+                    got_way[q] = jnp.where(here, way, got_way[q])
 
     group = lane // E
     own_mask = [jnp.full((E, L), is_own[q], jnp.int32) == 1 for q in range(PER)]
@@ -167,7 +246,7 @@
             at = pl.ds(pl.multiple_of(t * L, L), L)
             parts = []
             for q in range(PER):
-                got = rv[got_slot[q], :, at]
+                got = rv[got_way[q], got_slot[q], :, at]
                 if i == 1:
                     got = jnp.concatenate([got, pltpu.roll(got, E // 2 - 1, 0)], axis=0)
                 parts.append(jnp.where(own_mask[q], own[own_slot[q], :, at], got))
@@ -271,6 +350,7 @@
     assembled(1, put_u)
     send_faces(1, u, pack_all_z(u))
 
+    migrate(9, 11)
     wait_faces(0)
     b[pl.ds(first - 1, E, stride=ST), :] = hr[0, 0]
     b[pl.ds(first + E, E, stride=ST), :] = hr[0, 1]
@@ -300,6 +380,7 @@
 
     lax.fori_loop(0, E, coefs, 0)
 
+    migrate(11, len(steps) + lag)
     arrived(2)
 
     def put_a(y, plane):
@@ -402,9 +483,13 @@
     for x in range(E):
         res_out[x] = res[pl.ds(x, E, stride=E), :]
 
-    for i, (_, st, rv) in enumerate(fields):
-        for k in range(1, n_y):
-            migrate(i, k, st, rv).wait_send()
+    for i, part in steps:
+        for way in range(2):
+
+            @pl.when(sends(way))
+            def _():
+                hop(i, way, part, my_y + 1 - 2 * way).wait_send()
+
     for exchange in range(e + 1):
         for side in range(6):
 
@@ -421,8 +506,8 @@
     padded = pltpu.VMEM(((E + 2) * ST + 16, L), jnp.float32)
     faces = pltpu.VMEM((exchanges, 6, E, L), jnp.float32)
     own = pltpu.VMEM((PER,) + box, jnp.float32)
-    moved = pltpu.VMEM((n_y - 1,) + box, jnp.float32)
-    half = pltpu.VMEM((n_y - 1, E // 2, E * E), jnp.float32)
+    moved = pltpu.VMEM((2, n_y - 1) + box, jnp.float32)
+    half = pltpu.VMEM((2, n_y - 1, E // 2, E * E), jnp.float32)
     out = jax.ShapeDtypeStruct((E, E, L), jnp.float32)
     return pl.pallas_call(
         functools.partial(kernel, width),
@@ -439,8 +524,8 @@
         + [faces] * 2
         + [
             pltpu.SemaphoreType.DMA((4,)),
-            pltpu.SemaphoreType.DMA((4, n_y - 1)),
-            pltpu.SemaphoreType.DMA((4, n_y - 1)),
+            pltpu.SemaphoreType.DMA((4, 2, 5)),
+            pltpu.SemaphoreType.DMA((4, 2, 5)),
             pltpu.SemaphoreType.DMA((exchanges, 6)),
             pltpu.SemaphoreType.DMA((exchanges, 6)),
         ],

time: 76.7 us -> 111 us (1.45)
  Pallas kernels: 73.1 us -> 107 us
    pallas_call x1, Pallas kernels: 73.1 us -> 107 us  [per_device(): pl.pallas_call(functools.partial(kernel, width), out_shape=(out, out), in...]
where the time goes in v3:
time: 111 us
  Pallas kernels  107 us (96%)
  local copies, waits for them, and re-layouts  2.72 us (2%)
    pallas_call x1, Pallas kernels, per_device(): pl.pallas_call(functools.partial(kernel, width), out_shape=(out, out), in...  107 us
    unnamed x4, local copies, waits for them, and re-layouts  2.72 us

profile of v3, /device:TPU:0, one launch (start us, length us, event | category | flops | bytes accessed | tf_op | source)
XLA Modules:
  0.0 110.8 jit_solution(5119468839513608899)
XLA Ops:
  0.6 107.5 %shard_map.68 = (f32[32,32,128]{2,1,0:T(8,128)}, f32[32,32,128]{2,1,0:T(8,128)}) custom-call(s32[3,128]{1,0:T(4,128)} %corners.1, f32[4,32,1024]{2,1,0:T(8,128)} %sol_in.1, f32[4,32,1024]{2,1,0:T(8,128)} %rhs_in.1, f32[4,32,1024]{2,1,0:T(8,128)} %abs_in.1, f32[4,32,1024]{2,1,0:T(8,128)} %dif_in.1), custom_call_target="tpu_custom_call" | custom-call | flops 13107200 | bytes 3145728 | tf_op jit(solution)/shard_map/pallas_call | solution.py:512
  108.1 0.0 copy-start
  108.1 1.9 %copy.9 = f32[32,32,128]{2,1,0:T(8,128)} copy(f32[32,32,128]{2,1,0:T(8,128)} %get-tuple-element.4) | data formatting | bytes 1048576
  110.0 0.0 copy-done
  110.0 0.8 copy.10
Async XLA Ops:
  108.1 1.9 %copy-start = (f32[32,32,128]{2,1,0:T(8,128)S(1)}, f32[32,32,128]{2,1,0:T(8,128)}, u32[]{:S(2)}) copy-start(f32[32,32,128]{2,1,0:T(8,128)} %get-tuple-element.5) | copy-start | bytes 1572868

commit v4 on v3

--- a/solution.py
+++ b/solution.py
@@ -183,21 +183,20 @@
             hop(i, way, part, my_y - 1 + 2 * way).wait_recv()
 
     def pass_on(i, way, part):
-        rows = fields[i][1].shape[2]
-        if part < chunks[i]:
-            take_hop(i, way, part)
-            rows = rows // chunks[i]
-            for k in range(n_slot - 1):
-                fill(i, way, k, part * rows, rows)
-        else:
-            fill(i, way, n_slot - 1, 0, rows)
-
         @pl.when(sends(way))
         def _():
+            rows = fields[i][1].shape[2]
+            if part < chunks[i]:
+                take_hop(i, way, part)
+                rows = rows // chunks[i]
+                for k in range(n_slot - 1):
+                    fill(i, way, k, part * rows, rows)
+            else:
+                fill(i, way, n_slot - 1, 0, rows)
             hop(i, way, part, my_y + 1 - 2 * way).start()
 
     steps = [(i, part) for i in range(4) for part in range(chunks[i] + 1)]
-    lag = 2
+    lag = 3
 
     def migrate(first_step, last_step):
         for n in range(first_step, last_step):
@@ -213,6 +212,12 @@
 
     def arrived(i):
         for way in range(2):
+
+            @pl.when(jnp.logical_not(sends(way)))
+            def _():
+                for part in range(chunks[i]):
+                    take_hop(i, way, part)
+
             take_hop(i, way, chunks[i])
 
     migrate(0, 9)

time: 111 us -> 85.9 us (0.77)
  Pallas kernels: 107 us -> 82.4 us
    pallas_call x1, Pallas kernels: 107 us -> 82.4 us  [per_device(): pl.pallas_call(functools.partial(kernel, width), out_shape=(out, out), in...]
where the time goes in v4:
time: 85.9 us; the launch traced here: 85.7 us
  Pallas kernels  82.4 us (96%)
  local copies, waits for them, and re-layouts  2.72 us (3%)
    pallas_call x1, Pallas kernels, per_device(): pl.pallas_call(functools.partial(kernel, width), out_shape=(out, out), in...  82.4 us
    unnamed x4, local copies, waits for them, and re-layouts  2.72 us

profile of v4, /device:TPU:0, one launch (start us, length us, event | category | flops | bytes accessed | tf_op | source)
XLA Modules:
  0.0 85.7 jit_solution(15283960305158342502)
XLA Ops:
  0.6 82.4 %shard_map.68 = (f32[32,32,128]{2,1,0:T(8,128)}, f32[32,32,128]{2,1,0:T(8,128)}) custom-call(s32[3,128]{1,0:T(4,128)} %corners.1, f32[4,32,1024]{2,1,0:T(8,128)} %sol_in.1, f32[4,32,1024]{2,1,0:T(8,128)} %rhs_in.1, f32[4,32,1024]{2,1,0:T(8,128)} %abs_in.1, f32[4,32,1024]{2,1,0:T(8,128)} %dif_in.1), custom_call_target="tpu_custom_call" | custom-call | flops 13107200 | bytes 3145728 | tf_op jit(solution)/shard_map/pallas_call | solution.py:517
  83.0 0.0 copy-start
  83.0 1.9 %copy.9 = f32[32,32,128]{2,1,0:T(8,128)} copy(f32[32,32,128]{2,1,0:T(8,128)} %get-tuple-element.4) | data formatting | bytes 1048576
  84.9 0.0 copy-done
  84.9 0.8 copy.10
Async XLA Ops:
  83.0 1.9 %copy-start = (f32[32,32,128]{2,1,0:T(8,128)S(1)}, f32[32,32,128]{2,1,0:T(8,128)}, u32[]{:S(2)}) copy-start(f32[32,32,128]{2,1,0:T(8,128)} %get-tuple-element.5) | copy-start | bytes 1572868

commit v5 on v2

--- a/solution.py
+++ b/solution.py
@@ -76,8 +76,6 @@
         return me[axis] > 0 if step < 0 else me[axis] < width[axis] - 1
 
     hr[...] = jnp.zeros_like(hr)
-    b[...] = jnp.zeros_like(b)
-    u[...] = jnp.zeros_like(u)
 
     barrier = pltpu.get_barrier_semaphore()
     partners = n_y - 1
@@ -140,7 +138,8 @@
         )
 
     fields = ((own_b, st_b, rv_b), (own_u, st_u, rv_u), (own_a, st_a, rv_a), (own_f, st_f, rv_f))
-    for i, (own, st, rv) in enumerate(fields):
+    def send_boxes(i):
+        own, st, rv = fields[i]
         loads[i].wait()
         for k in range(1, n_y):
             box = own[send_slot[k - 1]]
@@ -152,6 +151,11 @@
         for k in range(1, n_y):
             migrate(i, k, st, rv).start()
 
+    for i in range(3):
+        send_boxes(i)
+    b[...] = jnp.zeros_like(b)
+    u[...] = jnp.zeros_like(u)
+
     def arrived(i):
         _, st, rv = fields[i]
         for k in range(1, n_y):
@@ -160,7 +164,7 @@
     group = lane // E
     own_mask = [jnp.full((E, L), is_own[q], jnp.int32) == 1 for q in range(PER)]
 
-    def assembled(i, put):
+    def assembled(i, put, carry=0):
         own, _, rv = fields[i]
 
         def columns(t, carry):
@@ -178,10 +182,10 @@
                         plane = jnp.where(
                             group == q, pltpu.roll(parts[q], (q - j) * E % L, 1), plane
                         )
-                put(t * PER + j, plane)
+                carry = put(t * PER + j, j, plane, carry)
             return carry
 
-        lax.fori_loop(0, E * E // L, columns, 0)
+        return lax.fori_loop(0, E * E // L, columns, carry)
 
     def at_plane(y):
         return pl.ds(pl.multiple_of(y * E, E), E)
@@ -257,19 +261,22 @@
 
     arrived(0)
 
-    def put_b(y, plane):
+    def put_b(y, j, plane, carry):
         b[padded(y), :] = plane
+        return carry
 
     assembled(0, put_b)
     send_faces(0, b, pack_all_z(b))
 
     arrived(1)
 
-    def put_u(y, plane):
+    def put_u(y, j, plane, carry):
         u[padded(y), :] = plane
+        return carry
 
     assembled(1, put_u)
     send_faces(1, u, pack_all_z(u))
+    send_boxes(3)
 
     wait_faces(0)
     b[pl.ds(first - 1, E, stride=ST), :] = hr[0, 0]
@@ -302,21 +309,16 @@
 
     arrived(2)
 
-    def put_a(y, plane):
+    def put_a(y, j, plane, carry):
         at = at_plane(y)
         total = plane + dia[at, :]
         inverse = 1.0 / total
         dia[at, :] = total
         inv[at, :] = inverse
         ezi[at, :] = ez[at, :] * inverse
+        return carry
 
     assembled(2, put_a)
-    arrived(3)
-
-    def put_f(y, plane):
-        f[at_plane(y), :] = plane
-
-    assembled(3, put_f)
 
     def neighbours(y):
         at = at_plane(y)
@@ -332,9 +334,44 @@
     high_y = pl.ds((E - 1) * E, E)
     top_y = pl.ds(E * E, E)
 
-    e = 1
+    def add_faces(e):
+        for at, term in (
+            (low_x, cxl[low_x, :] * hr[e, 0]),
+            (high_x, cxh[high_x, :] * hr[e, 1]),
+            (low_y, cy[low_y, :] * hr[e, 2]),
+            (high_y, cy[top_y, :] * hr[e, 3]),
+        ):
+            res[at, :] = res[at, :] + term
+
+    wait_faces(1)
+    first_halo = z_halo(1)
+
+    def first_sums(t, carry):
+        for j in range(4):
+            y = t * 4 + j
+            at = at_plane(y)
+            res[at, :] = neighbours(y)[1] + ez[at, :] * z_edge(first_halo, y)
+        return carry
+
+    lax.fori_loop(0, E // 4, first_sums, 0)
+    add_faces(1)
+    arrived(3)
+
+    def put_f(y, j, plane, face):
+        at = at_plane(y)
+        f[at, :] = plane
+        new = (plane + res[at, :]) * inv[at, :]
+        v = jnp.where(even if j % 2 == 0 else odd, new, u[padded(y), :])
+        u[padded(y), :] = v
+        return pack_z(y, v, face)
+
+    send_faces(2, u, assembled(3, put_f, zero))
+
+    e = 2
     for sweep in range(SWEEPS):
         for colour in (0, 1):
+            if sweep == 0 and colour == 0:
+                continue
             masks = (even, odd) if colour == 0 else (odd, even)
 
             def planes(t, carry):
@@ -382,13 +419,7 @@
     for x in range(E):
         sol_out[x] = u[pl.ds(first + x, E, stride=ST), :]
     wait_faces(e)
-    for at, term in (
-        (low_x, cxl[low_x, :] * hr[e, 0]),
-        (high_x, cxh[high_x, :] * hr[e, 1]),
-        (low_y, cy[low_y, :] * hr[e, 2]),
-        (high_y, cy[top_y, :] * hr[e, 3]),
-    ):
-        res[at, :] = res[at, :] + term
+    add_faces(e)
     last_halo = z_halo(e)
 
     def last_edges(t, carry):

time: 76.7 us -> 71.2 us (0.928)
  Pallas kernels: 73.1 us -> 67.7 us
    pallas_call x1, Pallas kernels: 73.1 us -> 67.7 us  [per_device(): pl.pallas_call(functools.partial(kernel, width), out_shape=(out, out), in...]
where the time goes in v5:
time: 71.2 us; the launch traced here: 71 us
  Pallas kernels  67.7 us (95%)
  local copies, waits for them, and re-layouts  2.72 us (4%)
    pallas_call x1, Pallas kernels, per_device(): pl.pallas_call(functools.partial(kernel, width), out_shape=(out, out), in...  67.7 us
    unnamed x4, local copies, waits for them, and re-layouts  2.72 us

profile of v5, /device:TPU:0, one launch (start us, length us, event | category | flops | bytes accessed | tf_op | source)
XLA Modules:
  0.0 71.0 jit_solution(11197524359799319768)
XLA Ops:
  0.6 67.7 %shard_map.68 = (f32[32,32,128]{2,1,0:T(8,128)}, f32[32,32,128]{2,1,0:T(8,128)}) custom-call(s32[3,128]{1,0:T(4,128)} %corners.1, f32[4,32,1024]{2,1,0:T(8,128)} %sol_in.1, f32[4,32,1024]{2,1,0:T(8,128)} %rhs_in.1, f32[4,32,1024]{2,1,0:T(8,128)} %abs_in.1, f32[4,32,1024]{2,1,0:T(8,128)} %dif_in.1), custom_call_target="tpu_custom_call" | custom-call | flops 13107200 | bytes 3145728 | tf_op jit(solution)/shard_map/pallas_call | solution.py:458
  68.3 0.0 copy-start
  68.3 1.9 %copy.9 = f32[32,32,128]{2,1,0:T(8,128)} copy(f32[32,32,128]{2,1,0:T(8,128)} %get-tuple-element.4) | data formatting | bytes 1048576
  70.2 0.0 copy-done
  70.2 0.8 %copy.10 = f32[32,32,128]{2,1,0:T(8,128)} copy(f32[32,32,128]{2,1,0:T(8,128)S(1)} %copy-done) | data formatting | bytes 1048576
Async XLA Ops:
  68.3 1.9 %copy-start = (f32[32,32,128]{2,1,0:T(8,128)S(1)}, f32[32,32,128]{2,1,0:T(8,128)}, u32[]{:S(2)}) copy-start(f32[32,32,128]{2,1,0:T(8,128)} %get-tuple-element.5) | copy-start | bytes 1572868

commit v6 on v4

--- a/solution.py
+++ b/solution.py
@@ -76,8 +76,6 @@
         return me[axis] > 0 if step < 0 else me[axis] < width[axis] - 1
 
     hr[...] = jnp.zeros_like(hr)
-    b[...] = jnp.zeros_like(b)
-    u[...] = jnp.zeros_like(u)
 
     barrier = pltpu.get_barrier_semaphore()
     partners = 0
@@ -163,7 +161,7 @@
     def receives(way):
         return jnp.where(way == 0, my_y > 0, my_y < n_y - 1)
 
-    def fill(i, way, k, start, rows):
+    def fill(i, way, k, start, rows, relays=True):
         own, st, rv = fields[i]
         held = jnp.where(way == 0, code[0][k], code[1][k])
         slot = jnp.where(held < PER, held, 0)
@@ -172,7 +170,7 @@
             box = jnp.where(odd_half, box[: E // 2], pltpu.roll(box[E // 2 :], 1, 0))
         else:
             box = own[slot, pl.ds(start, rows), :]
-        for r in range(n_slot - 1):
+        for r in range(n_slot - 1 if relays else 0):
             relayed = jnp.full((rows, E * E), held, jnp.int32) == PER + r
             box = jnp.where(relayed, rv[way, r, pl.ds(start, rows), :], box)
         st[way, k, pl.ds(start, rows), :] = box
@@ -182,7 +180,7 @@
         def _():
             hop(i, way, part, my_y - 1 + 2 * way).wait_recv()
 
-    def pass_on(i, way, part):
+    def pass_on(i, way, part, relays=True):
         @pl.when(sends(way))
         def _():
             rows = fields[i][1].shape[2]
@@ -192,23 +190,33 @@
                 for k in range(n_slot - 1):
                     fill(i, way, k, part * rows, rows)
             else:
-                fill(i, way, n_slot - 1, 0, rows)
+                fill(i, way, n_slot - 1, 0, rows, relays)
             hop(i, way, part, my_y + 1 - 2 * way).start()
 
     steps = [(i, part) for i in range(4) for part in range(chunks[i] + 1)]
-    lag = 3
-
-    def migrate(first_step, last_step):
-        for n in range(first_step, last_step):
-            if n < len(steps):
-                i, part = steps[n]
-                if part == 0:
-                    loads[i].wait()
-                if n == 0:
-                    pl.semaphore_wait(barrier, partners)
-                pass_on(i, inward, part)
-            if 0 <= n - lag < len(steps):
-                pass_on(steps[n - lag][0], outward, steps[n - lag][1])
+    lag = 2
+    ahead = n_y <= 4
+
+    def end_sends(i, parts):
+        @pl.when(jnp.logical_not(receives(inward)))
+        def _():
+            for part in parts:
+                pass_on(i, inward, part, relays=False)
+
+    def last_out(i):
+        if ahead:
+            pass_on(i, outward, chunks[i], relays=False)
+
+    def middle(first_step, last_step):
+        @pl.when(receives(inward))
+        def _():
+            for n in range(first_step, last_step):
+                if n < len(steps):
+                    pass_on(steps[n][0], inward, steps[n][1])
+                if 0 <= n - lag < len(steps):
+                    i, part = steps[n - lag]
+                    if not (ahead and part == chunks[i]):
+                        pass_on(i, outward, part)
 
     def arrived(i):
         for way in range(2):
@@ -220,7 +228,18 @@
 
             take_hop(i, way, chunks[i])
 
-    migrate(0, 9)
+    for i in range(3):
+        loads[i].wait()
+        if i == 0:
+            pl.semaphore_wait(barrier, partners)
+        end_sends(i, range(chunks[i] + 1))
+    last_out(0)
+    last_out(1)
+    middle(0, 7)
+    last_out(2)
+    middle(7, 9)
+    b[...] = jnp.zeros_like(b)
+    u[...] = jnp.zeros_like(u)
 
     own_slot = [jnp.int32(0)] * PER
     is_own = [jnp.int32(0)] * PER
@@ -244,7 +263,7 @@
     group = lane // E
     own_mask = [jnp.full((E, L), is_own[q], jnp.int32) == 1 for q in range(PER)]
 
-    def assembled(i, put):
+    def assembled(i, put, carry=0):
         own, _, rv = fields[i]
 
         def columns(t, carry):
@@ -262,10 +281,10 @@
                         plane = jnp.where(
                             group == q, pltpu.roll(parts[q], (q - j) * E % L, 1), plane
                         )
-                put(t * PER + j, plane)
+                carry = put(t * PER + j, j, plane, carry)
             return carry
 
-        lax.fori_loop(0, E * E // L, columns, 0)
+        return lax.fori_loop(0, E * E // L, columns, carry)
 
     def at_plane(y):
         return pl.ds(pl.multiple_of(y * E, E), E)
@@ -341,21 +360,30 @@
 
     arrived(0)
 
-    def put_b(y, plane):
+    def put_b(y, j, plane, carry):
         b[padded(y), :] = plane
+        return carry
 
     assembled(0, put_b)
     send_faces(0, b, pack_all_z(b))
 
+    loads[3].wait()
+    end_sends(3, (0,))
+    middle(9, 10)
+
     arrived(1)
 
-    def put_u(y, plane):
+    def put_u(y, j, plane, carry):
         u[padded(y), :] = plane
+        return carry
 
     assembled(1, put_u)
     send_faces(1, u, pack_all_z(u))
 
-    migrate(9, 11)
+    end_sends(3, (1, 2))
+    last_out(3)
+    middle(10, 11)
+
     wait_faces(0)
     b[pl.ds(first - 1, E, stride=ST), :] = hr[0, 0]
     b[pl.ds(first + E, E, stride=ST), :] = hr[0, 1]
@@ -385,24 +413,19 @@
 
     lax.fori_loop(0, E, coefs, 0)
 
-    migrate(11, len(steps) + lag)
+    middle(11, 12)
     arrived(2)
 
-    def put_a(y, plane):
+    def put_a(y, j, plane, carry):
         at = at_plane(y)
         total = plane + dia[at, :]
         inverse = 1.0 / total
         dia[at, :] = total
         inv[at, :] = inverse
         ezi[at, :] = ez[at, :] * inverse
+        return carry
 
     assembled(2, put_a)
-    arrived(3)
-
-    def put_f(y, plane):
-        f[at_plane(y), :] = plane
-
-    assembled(3, put_f)
 
     def neighbours(y):
         at = at_plane(y)
@@ -418,9 +441,45 @@
     high_y = pl.ds((E - 1) * E, E)
     top_y = pl.ds(E * E, E)
 
-    e = 1
+    def add_faces(e):
+        for at, term in (
+            (low_x, cxl[low_x, :] * hr[e, 0]),
+            (high_x, cxh[high_x, :] * hr[e, 1]),
+            (low_y, cy[low_y, :] * hr[e, 2]),
+            (high_y, cy[top_y, :] * hr[e, 3]),
+        ):
+            res[at, :] = res[at, :] + term
+
+    middle(12, len(steps) + lag)
+    wait_faces(1)
+    first_halo = z_halo(1)
+
+    def first_sums(t, carry):
+        for j in range(4):
+            y = t * 4 + j
+            at = at_plane(y)
+            res[at, :] = neighbours(y)[1] + ez[at, :] * z_edge(first_halo, y)
+        return carry
+
+    lax.fori_loop(0, E // 4, first_sums, 0)
+    add_faces(1)
+    arrived(3)
+
+    def put_f(y, j, plane, face):
+        at = at_plane(y)
+        f[at, :] = plane
+        new = (plane + res[at, :]) * inv[at, :]
+        v = jnp.where(even if j % 2 == 0 else odd, new, u[padded(y), :])
+        u[padded(y), :] = v
+        return pack_z(y, v, face)
+
+    send_faces(2, u, assembled(3, put_f, zero))
+
+    e = 2
     for sweep in range(SWEEPS):
         for colour in (0, 1):
+            if sweep == 0 and colour == 0:
+                continue
             masks = (even, odd) if colour == 0 else (odd, even)
 
             def planes(t, carry):
@@ -468,13 +527,7 @@
     for x in range(E):
         sol_out[x] = u[pl.ds(first + x, E, stride=ST), :]
     wait_faces(e)
-    for at, term in (
-        (low_x, cxl[low_x, :] * hr[e, 0]),
-        (high_x, cxh[high_x, :] * hr[e, 1]),
-        (low_y, cy[low_y, :] * hr[e, 2]),
-        (high_y, cy[top_y, :] * hr[e, 3]),
-    ):
-        res[at, :] = res[at, :] + term
+    add_faces(e)
     last_halo = z_halo(e)
 
     def last_edges(t, carry):

time: 85.9 us -> 70.5 us (0.82)
  Pallas kernels: 82.4 us -> 67 us
    pallas_call x1, Pallas kernels: 82.4 us -> 67 us  [per_device(): pl.pallas_call(functools.partial(kernel, width), out_shape=(out, out), in...]
where the time goes in v6:
time: 70.5 us; the launch traced here: 70.3 us
  Pallas kernels  67 us (95%)
  local copies, waits for them, and re-layouts  2.72 us (4%)
    pallas_call x1, Pallas kernels, per_device(): pl.pallas_call(functools.partial(kernel, width), out_shape=(out, out), in...  67 us
    unnamed x4, local copies, waits for them, and re-layouts  2.72 us

profile of v6, /device:TPU:0, one launch (start us, length us, event | category | flops | bytes accessed | tf_op | source)
XLA Modules:
  0.0 70.3 jit_solution(2442238259610120878)
XLA Ops:
  0.6 67.0 %shard_map.68 = (f32[32,32,128]{2,1,0:T(8,128)}, f32[32,32,128]{2,1,0:T(8,128)}) custom-call(s32[3,128]{1,0:T(4,128)} %corners.1, f32[4,32,1024]{2,1,0:T(8,128)} %sol_in.1, f32[4,32,1024]{2,1,0:T(8,128)} %rhs_in.1, f32[4,32,1024]{2,1,0:T(8,128)} %abs_in.1, f32[4,32,1024]{2,1,0:T(8,128)} %dif_in.1), custom_call_target="tpu_custom_call" | custom-call | flops 13107200 | bytes 3145728 | tf_op jit(solution)/shard_map/pallas_call | solution.py:570
  67.6 0.0 copy-start
  67.6 1.9 %copy.9 = f32[32,32,128]{2,1,0:T(8,128)} copy(f32[32,32,128]{2,1,0:T(8,128)} %get-tuple-element.4) | data formatting | bytes 1048576
  69.5 0.0 copy-done
  69.6 0.8 %copy.10 = f32[32,32,128]{2,1,0:T(8,128)} copy(f32[32,32,128]{2,1,0:T(8,128)S(1)} %copy-done) | data formatting | bytes 1048576
Async XLA Ops:
  67.6 1.9 %copy-start = (f32[32,32,128]{2,1,0:T(8,128)S(1)}, f32[32,32,128]{2,1,0:T(8,128)}, u32[]{:S(2)}) copy-start(f32[32,32,128]{2,1,0:T(8,128)} %get-tuple-element.5) | copy-start | bytes 1572868

commit v7 on v6

--- a/solution.py
+++ b/solution.py
@@ -63,13 +63,21 @@
     my_y = me["gy"]
 
     loads = [
-        pltpu.make_async_copy(src, dst, in_sem.at[i])
+        [
+            pltpu.make_async_copy(src.at[q], dst.at[q], in_sem.at[i, q])
+            for q in range(PER)
+        ]
         for i, (src, dst) in enumerate(
             ((dif_in, own_b), (sol_in, own_u), (abs_in, own_a), (rhs_in, own_f))
         )
     ]
-    for load in loads:
-        load.start()
+    for field_loads in loads:
+        for load in field_loads:
+            load.start()
+
+    def loaded(i):
+        for load in loads[i]:
+            load.wait()
 
     def exists(side):
         axis, step = SIDES[side]
@@ -136,7 +144,7 @@
     odd_half = (wide_row + wide_lane // E + wide_lane) % 2 == 1
 
     fields = ((own_b, st_b, rv_b), (own_u, st_u, rv_u), (own_a, st_a, rv_a), (own_f, st_f, rv_f))
-    chunks = (4, 1, 2, 2)
+    chunks = (4, 1, 4, 4)
 
     def part_of(ref, i, way, part):
         if part == chunks[i]:
@@ -229,7 +237,7 @@
             take_hop(i, way, chunks[i])
 
     for i in range(3):
-        loads[i].wait()
+        loaded(i)
         if i == 0:
             pl.semaphore_wait(barrier, partners)
         end_sends(i, range(chunks[i] + 1))
@@ -237,7 +245,7 @@
     last_out(1)
     middle(0, 7)
     last_out(2)
-    middle(7, 9)
+    middle(7, 11)
     b[...] = jnp.zeros_like(b)
     u[...] = jnp.zeros_like(u)
 
@@ -367,9 +375,9 @@
     assembled(0, put_b)
     send_faces(0, b, pack_all_z(b))
 
-    loads[3].wait()
-    end_sends(3, (0,))
-    middle(9, 10)
+    loaded(3)
+    end_sends(3, (0, 1))
+    middle(11, 12)
 
     arrived(1)
 
@@ -380,9 +388,9 @@
     assembled(1, put_u)
     send_faces(1, u, pack_all_z(u))
 
-    end_sends(3, (1, 2))
+    end_sends(3, (2, 3, 4))
     last_out(3)
-    middle(10, 11)
+    middle(12, 14)
 
     wait_faces(0)
     b[pl.ds(first - 1, E, stride=ST), :] = hr[0, 0]
@@ -413,7 +421,7 @@
 
     lax.fori_loop(0, E, coefs, 0)
 
-    middle(11, 12)
+    middle(14, 16)
     arrived(2)
 
     def put_a(y, j, plane, carry):
@@ -450,7 +458,7 @@
         ):
             res[at, :] = res[at, :] + term
 
-    middle(12, len(steps) + lag)
+    middle(16, len(steps) + lag)
     wait_faces(1)
     first_halo = z_halo(1)
 
@@ -581,7 +589,7 @@
         + [field] * 4
         + [faces] * 2
         + [
-            pltpu.SemaphoreType.DMA((4,)),
+            pltpu.SemaphoreType.DMA((4, PER)),
             pltpu.SemaphoreType.DMA((4, 2, 5)),
             pltpu.SemaphoreType.DMA((4, 2, 5)),
             pltpu.SemaphoreType.DMA((exchanges, 6)),

time: 70.5 us -> 69.2 us (0.982)
  Pallas kernels: 67 us -> 65.7 us
    pallas_call x1, Pallas kernels: 67 us -> 65.7 us  [per_device(): pl.pallas_call(functools.partial(kernel, width), out_shape=(out, out), in...]
where the time goes in v7:
time: 69.2 us; the launch traced here: 69.1 us
  Pallas kernels  65.7 us (95%)
  local copies, waits for them, and re-layouts  2.72 us (4%)
    pallas_call x1, Pallas kernels, per_device(): pl.pallas_call(functools.partial(kernel, width), out_shape=(out, out), in...  65.7 us
    unnamed x4, local copies, waits for them, and re-layouts  2.72 us

profile of v7, /device:TPU:0, one launch (start us, length us, event | category | flops | bytes accessed | tf_op | source)
XLA Modules:
  0.0 69.1 jit_solution(1049638074394565350)
XLA Ops:
  0.6 65.7 %shard_map.68 = (f32[32,32,128]{2,1,0:T(8,128)}, f32[32,32,128]{2,1,0:T(8,128)}) custom-call(s32[3,128]{1,0:T(4,128)} %corners.1, f32[4,32,1024]{2,1,0:T(8,128)} %sol_in.1, f32[4,32,1024]{2,1,0:T(8,128)} %rhs_in.1, f32[4,32,1024]{2,1,0:T(8,128)} %abs_in.1, f32[4,32,1024]{2,1,0:T(8,128)} %dif_in.1), custom_call_target="tpu_custom_call" | custom-call | flops 13107200 | bytes 3145728 | tf_op jit(solution)/shard_map/pallas_call | solution.py:578
  66.3 0.0 copy-start
  66.3 1.9 %copy.9 = f32[32,32,128]{2,1,0:T(8,128)} copy(f32[32,32,128]{2,1,0:T(8,128)} %get-tuple-element.4) | data formatting | bytes 1048576
  68.3 0.0 copy-done
  68.3 0.8 %copy.10 = f32[32,32,128]{2,1,0:T(8,128)} copy(f32[32,32,128]{2,1,0:T(8,128)S(1)} %copy-done) | data formatting | bytes 1048576
Async XLA Ops:
  66.3 1.9 %copy-start = (f32[32,32,128]{2,1,0:T(8,128)S(1)}, f32[32,32,128]{2,1,0:T(8,128)}, u32[]{:S(2)}) copy-start(f32[32,32,128]{2,1,0:T(8,128)} %get-tuple-element.5) | copy-start | bytes 1572868

commit v8 on v7

--- a/solution.py
+++ b/solution.py
@@ -23,8 +23,8 @@
     rhs_in,
     abs_in,
     dif_in,
-    sol_out,
-    res_out,
+    sol_hbm,
+    res_hbm,
     own_b,
     own_u,
     own_a,
@@ -52,6 +52,9 @@
     ezi,
     hs,
     hr,
+    sol_out,
+    res_out,
+    out_sem,
     in_sem,
     ms_sem,
     mr_sem,
@@ -534,6 +537,8 @@
     lax.fori_loop(0, E // 4, residual, 0)
     for x in range(E):
         sol_out[x] = u[pl.ds(first + x, E, stride=ST), :]
+    stores = [pltpu.make_async_copy(sol_out, sol_hbm, out_sem.at[4])]
+    stores[0].start()
     wait_faces(e)
     add_faces(e)
     last_halo = z_halo(e)
@@ -548,6 +553,12 @@
     lax.fori_loop(0, E // 4, last_edges, 0)
     for x in range(E):
         res_out[x] = res[pl.ds(x, E, stride=E), :]
+        if x % 8 == 7:
+            piece = pl.ds(x - 7, 8)
+            stores.append(
+                pltpu.make_async_copy(res_out.at[piece], res_hbm.at[piece], out_sem.at[x // 8])
+            )
+            stores[-1].start()
 
     for i, part in steps:
         for way in range(2):
@@ -555,6 +566,9 @@
             @pl.when(sends(way))
             def _():
                 hop(i, way, part, my_y + 1 - 2 * way).wait_send()
+
+    for store in stores:
+        store.wait()
 
     for exchange in range(e + 1):
         for side in range(6):
@@ -580,7 +594,7 @@
         out_shape=(out, out),
         in_specs=[pl.BlockSpec(memory_space=pltpu.SMEM)]
         + [pl.BlockSpec(memory_space=pl.ANY)] * 4,
-        out_specs=(pl.BlockSpec(memory_space=pltpu.VMEM),) * 2,
+        out_specs=(pl.BlockSpec(memory_space=pl.ANY),) * 2,
         scratch_shapes=[own] * 4
         + [moved, half, moved, moved] * 2
         + [padded, padded]
@@ -588,6 +602,8 @@
         + [pltpu.VMEM(((E + 1) * E, L), jnp.float32)]
         + [field] * 4
         + [faces] * 2
+        + [pltpu.VMEM((E, E, L), jnp.float32)] * 2
+        + [pltpu.SemaphoreType.DMA((5,))]
         + [
             pltpu.SemaphoreType.DMA((4, PER)),
             pltpu.SemaphoreType.DMA((4, 2, 5)),

time: 69.2 us -> 68.9 us (level)
  no operation moved by 1% of the time
where the time goes in v8:
time: 68.9 us; the launch traced here: 68.7 us
  Pallas kernels  65.3 us (95%)
  local copies, waits for them, and re-layouts  2.72 us (4%)
    pallas_call x1, Pallas kernels, per_device(): pl.pallas_call(functools.partial(kernel, width), out_shape=(out, out), in...  65.3 us
    unnamed x4, local copies, waits for them, and re-layouts  2.72 us

profile of v8, /device:TPU:0, one launch (start us, length us, event | category | flops | bytes accessed | tf_op | source)
XLA Modules:
  0.0 68.7 jit_solution(593051944979356361)
XLA Ops:
  0.6 65.3 %shard_map.68 = (f32[32,32,128]{2,1,0:T(8,128)}, f32[32,32,128]{2,1,0:T(8,128)}) custom-call(s32[3,128]{1,0:T(4,128)} %corners.1, f32[4,32,1024]{2,1,0:T(8,128)} %sol_in.1, f32[4,32,1024]{2,1,0:T(8,128)} %rhs_in.1, f32[4,32,1024]{2,1,0:T(8,128)} %abs_in.1, f32[4,32,1024]{2,1,0:T(8,128)} %dif_in.1), custom_call_target="tpu_custom_call" | custom-call | flops 13107200 | bytes 3145728 | tf_op jit(solution)/shard_map/pallas_call | solution.py:592
  66.0 0.0 copy-start
  66.0 1.9 %copy.9 = f32[32,32,128]{2,1,0:T(8,128)} copy(f32[32,32,128]{2,1,0:T(8,128)} %get-tuple-element.4) | data formatting | bytes 1048576
  67.9 0.0 copy-done
  67.9 0.8 %copy.10 = f32[32,32,128]{2,1,0:T(8,128)} copy(f32[32,32,128]{2,1,0:T(8,128)S(1)} %copy-done) | data formatting | bytes 1048576
Async XLA Ops:
  66.0 1.9 %copy-start = (f32[32,32,128]{2,1,0:T(8,128)S(1)}, f32[32,32,128]{2,1,0:T(8,128)}, u32[]{:S(2)}) copy-start(f32[32,32,128]{2,1,0:T(8,128)} %get-tuple-element.5) | copy-start | bytes 1572868

commit v9 on v8

--- a/solution.py
+++ b/solution.py
@@ -205,7 +205,7 @@
             hop(i, way, part, my_y + 1 - 2 * way).start()
 
     steps = [(i, part) for i in range(4) for part in range(chunks[i] + 1)]
-    lag = 2
+    lag = 1
     ahead = n_y <= 4
 
     def end_sends(i, parts):

time: 68.9 us -> 75.7 us (1.099)
  Pallas kernels: 65.3 us -> 72.2 us
    pallas_call x1, Pallas kernels: 65.3 us -> 72.2 us  [per_device(): pl.pallas_call(functools.partial(kernel, width), out_shape=(out, out), in...]
where the time goes in v9:
time: 75.7 us; the launch traced here: 75.6 us
  Pallas kernels  72.2 us (95%)
  local copies, waits for them, and re-layouts  2.72 us (4%)
    pallas_call x1, Pallas kernels, per_device(): pl.pallas_call(functools.partial(kernel, width), out_shape=(out, out), in...  72.2 us
    unnamed x4, local copies, waits for them, and re-layouts  2.72 us

profile of v9, /device:TPU:0, one launch (start us, length us, event | category | flops | bytes accessed | tf_op | source)
XLA Modules:
  0.0 75.6 jit_solution(10823802306008712758)
XLA Ops:
  0.6 72.2 %shard_map.68 = (f32[32,32,128]{2,1,0:T(8,128)}, f32[32,32,128]{2,1,0:T(8,128)}) custom-call(s32[3,128]{1,0:T(4,128)} %corners.1, f32[4,32,1024]{2,1,0:T(8,128)} %sol_in.1, f32[4,32,1024]{2,1,0:T(8,128)} %rhs_in.1, f32[4,32,1024]{2,1,0:T(8,128)} %abs_in.1, f32[4,32,1024]{2,1,0:T(8,128)} %dif_in.1), custom_call_target="tpu_custom_call" | custom-call | flops 13107200 | bytes 3145728 | tf_op jit(solution)/shard_map/pallas_call | solution.py:592
  72.8 0.0 copy-start
  72.8 1.9 %copy.9 = f32[32,32,128]{2,1,0:T(8,128)} copy(f32[32,32,128]{2,1,0:T(8,128)} %get-tuple-element.4) | data formatting | bytes 1048576
  74.8 0.0 copy-done
  74.8 0.8 %copy.10 = f32[32,32,128]{2,1,0:T(8,128)} copy(f32[32,32,128]{2,1,0:T(8,128)S(1)} %copy-done) | data formatting | bytes 1048576
Async XLA Ops:
  72.8 1.9 %copy-start = (f32[32,32,128]{2,1,0:T(8,128)S(1)}, f32[32,32,128]{2,1,0:T(8,128)}, u32[]{:S(2)}) copy-start(f32[32,32,128]{2,1,0:T(8,128)} %get-tuple-element.5) | copy-start | bytes 1572868
